TPU v7x, 32 devices: a whole 2x2x4 slice. The times are simulated.
32 devices in a mesh: tile: 16 (over z, y, core), scan: 2 (over x).
Axes of the slice: x: 2, y: 2, z: 4, core: 2. Of those that a mesh axis runs over, the one named last changes fastest.
Arguments:
- object_slab: float32 [2, 2, 1024, 512], P(None, None, 'tile', 'scan'), may hold values from -6 to 6
- probe_wave: bfloat16 [2, 512, 512], P(None, None, 'scan'), may hold values from -6 to 6
- amplitudes: float32 [32, 512, 512], P('tile', 'scan'), may hold values from 0.2 to 2
- row_offsets: int32 [32], P('tile'), may hold values from 0 to 63
- position_counts: int32 [16], P('tile'), may hold values from 0 to 2, as said below
Outputs:
- object_grad: float32 [2, 2, 1024, 512], P(None, None, 'tile', 'scan')
Inputs may be any that keep to these rules, and one draw needn't show every extreme that they name: position_counts is 1 to 2 on the first 8 tiles, equal to 2 on at least one of them, and 0 on the last 8 tiles.
All inputs are finite; a program needn't handle non-finite values.
Results may differ from a plain program's by a relative error of at most 0.0065.
Values may be sent and summed in bfloat16 or wider, within the bound.
No kernel may reach another device: no remote copies, remote signals or barrier semaphores. Data moves between devices by JAX's collectives and lax.ppermute only.
A program may use at most 64 MiB of HBM per device.

v0:
```python
import functools
import math

import jax
import jax.numpy as jnp
import ml_dtypes
import numpy as np
from jax import lax
from jax.experimental import pallas as pl
from jax.experimental.pallas import tpu as pltpu
from jax.sharding import PartitionSpec as P

fresnel = 0.5
smooth = 1.0
bf16 = jnp.bfloat16
f32 = jnp.float32


def tables(size):
    index = np.arange(size)
    angles = 2.0 * np.pi / size * (index[:, None] * index[None, :] % size)
    base = np.exp(1j * angles)
    far = np.conj(base) / math.sqrt(size)
    centred = np.where(index < size // 2, index, index - size).astype(np.float64)
    kernel = np.exp(-1j * np.pi * fresnel / size * centred * centred)
    near = (base * kernel[None, :]) @ np.conj(base).T / size

    def parts(table):
        stacked = np.stack([table.real, table.imag])
        return jnp.asarray(stacked.astype(ml_dtypes.bfloat16))

    order = np.concatenate([index[0::2], index[1::2]])
    return parts(far[order]), parts(far[:, order]), parts(near)


def three(table, conjugate):
    real, imag = table
    return (real, -imag, imag) if conjugate else (real, imag, -imag)


def left(table, conjugate, wave):
    real, plus, minus = three(table, conjugate)
    top = jnp.concatenate([real, minus], axis=1)
    bottom = jnp.concatenate([plus, real], axis=1)
    return (
        jnp.dot(top, wave, preferred_element_type=f32),
        jnp.dot(bottom, wave, preferred_element_type=f32),
    )


def right(table, conjugate, wave):
    real, plus, minus = three(table, conjugate)
    real_side = jnp.concatenate([real, minus], axis=0)
    imag_side = jnp.concatenate([plus, real], axis=0)
    return (
        jnp.dot(wave, real_side, preferred_element_type=f32),
        jnp.dot(wave, imag_side, preferred_element_type=f32),
    )


def one_hot(size, hit):
    row = lax.broadcasted_iota(jnp.int32, (size, size), 0)
    col = lax.broadcasted_iota(jnp.int32, (size, size), 1)
    return jnp.where(hit(row, col), 1.0, 0.0).astype(bf16)


def notes_of(span, slots, ref):
    rows = ref.shape[0]
    values = ref[rows - 16 : rows, 0:128].astype(f32)
    row = lax.broadcasted_iota(jnp.int32, values.shape, 0)
    col = lax.broadcasted_iota(jnp.int32, values.shape, 1)

    def note(at):
        return jnp.sum(jnp.where((row == 0) & (col == at), values, 0.0)).astype(jnp.int32)

    tile, slot = lax.axis_index("tile"), lax.axis_index("scan")
    ahead = span // 2
    home = (tile >= ahead) & (tile < lax.axis_size("tile") - ahead)
    live = home & (slot < note(slots))
    return note(jnp.minimum(slot, slots - 1)), live, slot, lax.rem(tile, 2)


def in_order(size, slot, measured, amps):
    half = size // 2
    for number, piece in enumerate(measured):
        rows = size // len(measured)
        at = pl.multiple_of(jnp.where(slot == number, 0, size - rows), rows)
        amps[pl.ds(at, rows), :] = piece[0:rows, :]

    def frequency(place, natural):
        return natural == jnp.where(place < half, 2 * place, 2 * (place - half) + 1)

    rows_first = jnp.dot(one_hot(size, frequency), amps[...], preferred_element_type=f32)
    return jnp.dot(
        rows_first.astype(bf16),
        one_hot(size, lambda row, col: frequency(col, row)),
        preferred_element_type=f32,
    )


def roll_kernel(size, span, slots, notes, far_rows, far_cols, *refs):
    pieces, (probe_out, near_side, far_side) = refs[:-3], refs[-3:]
    offset, _, slot, _ = notes_of(span, slots, notes)
    half = size // 2

    def moved(to, source):
        gap = to - source - offset
        return (gap == 0) | (gap == -size)

    down = one_hot(size, moved)
    across = one_hot(size, lambda row, col: moved(col, row))
    for c in range(2):
        near_side[c] = jnp.dot(
            far_rows[c], across[:, :half], preferred_element_type=f32
        ).astype(bf16)
        far_side[c] = jnp.dot(down[:half], far_cols[c], preferred_element_type=f32).astype(bf16)
    for c in range(2):
        done = 0
        for piece in pieces:
            turned = jnp.dot(down, piece[c], preferred_element_type=f32).astype(bf16)
            width = turned.shape[1]
            if len(pieces) == 2:
                at = pl.multiple_of(jnp.where(slot == done, 0, width), width)
                probe_out[c, :, pl.ds(at, width)] = turned
                done += 1
            else:
                probe_out[c, :, done : done + width] = turned
                done += width


def rolled(pieces, far_rows, far_cols, notes, size, span, slots):
    whole = pl.BlockSpec(memory_space=pltpu.VMEM)
    return pl.pallas_call(
        functools.partial(roll_kernel, size, span, slots),
        out_shape=[
            jax.ShapeDtypeStruct((2, size, size), bf16),
            jax.ShapeDtypeStruct((2, size, size // 2), bf16),
            jax.ShapeDtypeStruct((2, size // 2, size), bf16),
        ],
        in_specs=[whole] * (3 + len(pieces)),
        out_specs=[whole] * 3,
        compiler_params=pltpu.CompilerParams(vmem_limit_bytes=16 * 1024 * 1024),
        cost_estimate=pl.CostEstimate(
            flops=64 * size**3, bytes_accessed=24 * size * size, transcendentals=0
        ),
        name="rolled",
    )(notes, far_rows, far_cols, *pieces)


def tile_access(span, tile_rows, offset, core, mine, theirs):
    parts, _, _, _, width = mine.shape[1:]
    early = lax.broadcasted_iota(jnp.int32, (tile_rows, width), 0) < offset

    def place(k):
        return k // 2 if k % 2 == 0 else k // 2 + core

    def piece(k, h, s, c):
        source = mine if k % 2 == 0 else theirs
        return source[place(k), h, s, c].astype(f32)

    def patch(s, c):
        rows = []
        for k in range(span):
            blocks = [piece(k, h, s, c) for h in range(parts)]
            if k == 0:
                blocks = [jnp.where(early, piece(span, h, s, c), blocks[h]) for h in range(parts)]
            rows.append(jnp.concatenate(blocks, axis=1))
        return jnp.concatenate(rows, axis=0)

    return early, place, patch


def put_rows(rows_buf, pair):
    size = rows_buf.shape[1]
    for c in range(2):
        rows_buf[c * size : (c + 1) * size, :] = pair[c].astype(bf16)


def put_cols(cols_buf, pair):
    size = cols_buf.shape[0]
    for c in range(2):
        cols_buf[:, c * size : (c + 1) * size] = pair[c].astype(bf16)


def put_row_halves(rows_buf, first, second):
    half = rows_buf.shape[1] // 2
    for number, wave in enumerate((*first, *second)):
        rows_buf[number * half : (number + 1) * half, :] = wave.astype(bf16)


def put_col_halves(cols_buf, first, second):
    half = cols_buf.shape[0] // 2
    for number, wave in enumerate((*first, *second)):
        cols_buf[:, number * half : (number + 1) * half] = wave.astype(bf16)


def pair_of(ref):
    return ref[0].astype(f32), ref[1].astype(f32)


def parts_of(ref, rows, cols):
    return ref[0, rows, cols], ref[1, rows, cols]


def both(first, second, axis):
    return [jnp.concatenate([a, b], axis=axis) for a, b in zip(first, second)]


def plus(first, second):
    return [a + b for a, b in zip(first, second)]


def less(first, second):
    return [a - b for a, b in zip(first, second)]


def forth_kernel(
    size, span, slots, tile_rows, notes, mine, theirs, far_cols, near, probe, far_near,
    psi2, field, rows_buf, cols_buf,
):
    half = size // 2
    low, high, everything = slice(0, half), slice(half, size), slice(None)
    offset, live, _, core = notes_of(span, slots, notes)

    @pl.when(live)
    def _():
        _, _, patch = tile_access(span, tile_rows, offset, core, mine, theirs)
        near_parts = parts_of(near, everything, everything)
        pr, pi = pair_of(probe)
        ar, ai = patch(0, 0), patch(0, 1)
        put_rows(rows_buf, (pr * ar - pi * ai, pr * ai + pi * ar))
        put_cols(cols_buf, left(near_parts, False, rows_buf[...]))
        two = right(near_parts, False, cols_buf[...])
        psi2[0] = two[0].astype(bf16)
        psi2[1] = two[1].astype(bf16)
        wr, wi = pair_of(psi2)
        br, bi = patch(1, 0), patch(1, 1)
        wave_exit = (wr * br - wi * bi, wr * bi + wi * br)
        top, bottom = [x[low] for x in wave_exit], [x[high] for x in wave_exit]
        put_row_halves(rows_buf, plus(top, bottom), less(top, bottom))
        half2 = both(
            left(parts_of(far_near, low, everything), False, rows_buf[0:size, :]),
            left(parts_of(far_near, high, everything), False, rows_buf[size : 2 * size, :]),
            0,
        )
        top, bottom = [x[:, low] for x in half2], [x[:, high] for x in half2]
        put_col_halves(cols_buf, plus(top, bottom), less(top, bottom))
        for cols, source in ((low, cols_buf[:, 0:size]), (high, cols_buf[:, size : 2 * size])):
            fr, fi = right(parts_of(far_cols, low, cols), False, source)
            field[0, :, cols] = fr
            field[1, :, cols] = fi


def back_kernel(
    size, span, slots, tile_rows, notes, mine, theirs, far_rows, near, probe, far_far, psi2, field, *refs,
):
    measured, (keep, send, rows_buf, cols_buf) = refs[:-4], refs[-4:]
    offset, live, slot, core = notes_of(span, slots, notes)
    parts, _, _, _, width = keep.shape[1:]
    half = size // 2
    low, high, everything = slice(0, half), slice(half, size), slice(None)

    @pl.when(live)
    def _():
        early, place, patch = tile_access(span, tile_rows, offset, core, mine, theirs)

        def put_term(s, c, term):
            for k in range(span):
                for h in range(parts):
                    block = term[
                        k * tile_rows : (k + 1) * tile_rows, h * width : (h + 1) * width
                    ]
                    if k == 0:
                        keep[place(span), h, s, c] = jnp.where(early, block, 0.0).astype(bf16)
                        block = jnp.where(early, 0.0, block)
                    target = keep if k % 2 == 0 else send
                    target[place(k), h, s, c] = block.astype(bf16)

        amps = in_order(size, slot, measured, cols_buf.at[:, 0:size])
        chis = []
        for cols in (low, high):
            fr, fi = field[0, :, cols], field[1, :, cols]
            keeping = 1.0 - amps[:, cols] * lax.rsqrt(fr * fr + fi * fi + smooth)
            chis.append((fr * keeping, fi * keeping))
        put_col_halves(cols_buf, *chis)
        even = right(parts_of(far_rows, low, low), True, cols_buf[:, 0:size])
        odd = right(parts_of(far_rows, high, low), True, cols_buf[:, size : 2 * size])
        back1 = both(plus(even, odd), less(even, odd), 1)
        put_row_halves(rows_buf, [x[low] for x in back1], [x[high] for x in back1])
        even = left(parts_of(far_far, everything, low), True, rows_buf[0:size, :])
        odd = left(parts_of(far_far, everything, high), True, rows_buf[size : 2 * size, :])
        er, ei = both(plus(even, odd), less(even, odd), 0)
        br, bi = patch(1, 0), patch(1, 1)
        put_cols(cols_buf, (br * er + bi * ei, br * ei - bi * er))
        wr, wi = pair_of(psi2)
        put_term(1, 0, wr * er + wi * ei)
        put_term(1, 1, wr * ei - wi * er)
        near_parts = parts_of(near, everything, everything)
        put_rows(rows_buf, right(near_parts, True, cols_buf[...]))
        gr, gi = left(near_parts, True, rows_buf[...])
        pr, pi = pair_of(probe)
        put_term(0, 0, pr * gr + pi * gi)
        put_term(0, 1, pr * gi - pi * gr)
        send[(1 - core) * (span // 2)] = jnp.zeros(send.shape[1:], bf16)

    @pl.when(jnp.logical_not(live))
    def _():
        keep[...] = jnp.zeros(keep.shape, bf16)
        send[...] = jnp.zeros(send.shape, bf16)


def small_call(kernel, out_shape, scalars, values, name):
    inside = pl.BlockSpec(memory_space=pltpu.VMEM)
    return pl.pallas_call(
        kernel,
        out_shape=out_shape,
        in_specs=[pl.BlockSpec(memory_space=pltpu.SMEM)] * len(scalars) + [inside] * len(values),
        out_specs=jax.tree.map(lambda _: inside, out_shape),
        compiler_params=pltpu.CompilerParams(vmem_limit_bytes=12 * 1024 * 1024),
        cost_estimate=pl.CostEstimate(flops=0, bytes_accessed=1 << 20, transcendentals=0),
        name=name,
    )(*scalars, *values)


def placed(values, place_of, name):
    def kernel(*refs):
        for number, value in enumerate(refs[:-1]):
            refs[-1][place_of(number)] = value[...]

    shape = jax.ShapeDtypeStruct((len(values),) + values[0].shape, values[0].dtype)
    return small_call(kernel, shape, [], values, name)


def amplitude_messages(amplitudes, row_offsets, position_counts):
    slots, rows, size = amplitudes.shape

    def kernel(offsets, counts, amps, straight, crossed):
        slot = lax.axis_index("scan")
        straight[0:rows, :] = amps[slot].astype(bf16)
        crossed[...] = amps[1 - slot].astype(bf16)
        at = lax.broadcasted_iota(jnp.int32, (16, size), 1)
        notes = jnp.where(at == slots, counts[0].astype(f32), 0.0)
        for number in range(slots):
            notes = jnp.where(at == number, offsets[number].astype(f32), notes)
        straight[rows : rows + 16, :] = notes.astype(bf16)

    shapes = [jax.ShapeDtypeStruct((n, size), bf16) for n in (rows + 16, rows)]
    return small_call(kernel, shapes, [row_offsets, position_counts], [amplitudes], "messages")


def group(number):
    unit, flip = ((4, 0), (2, 1), (2, 2), (2, 3), (4, 4))[number]
    odd = lax.rem(lax.axis_index("tile") // unit, 2) == 1
    return jnp.where(odd, flip, 4 - flip)


def merged_messages(keep, got):
    def kernel(keep, got, *outs):
        for number, out in enumerate(outs):
            at = group(number)
            out[...] = (keep[at].astype(f32) + got[at].astype(f32)).astype(bf16)

    return small_call(kernel, [jax.ShapeDtypeStruct(keep.shape[1:], bf16)] * 5, [], [keep, got], "merge")


def merged_in_halves(keep, got):
    def kernel(keep, got, near_with, next_with, next_across, middle, half_own, half_away):
        def chunk(number, *half):
            at = (group(number), *half)
            return keep[at].astype(f32) + got[at].astype(f32)

        slot = lax.axis_index("scan")
        half_own[...] = chunk(3, slot)
        half_away[...] = chunk(3, 1 - slot).astype(bf16)
        for out, number in ((near_with, 1), (next_with, 0), (next_across, 4), (middle, 2)):
            out[...] = chunk(number).astype(bf16)

    whole = jax.ShapeDtypeStruct(keep.shape[1:], bf16)
    halves = [jax.ShapeDtypeStruct(keep.shape[2:], kind) for kind in (f32, bf16)]
    return small_call(kernel, [whole] * 4 + halves, [], [keep, got], "merge")


def summed(own, got):
    def kernel(own, got, out):
        out[...] = (own[...] + got[...].astype(f32)).astype(bf16)

    return small_call(kernel, jax.ShapeDtypeStruct(own.shape, bf16), [], [own, got], "near")


def halves_of_sum(values):
    def kernel(*refs):
        (own, away), slot = refs[-2:], lax.axis_index("scan")

        def half(h):
            return sum(ref[h].astype(f32) for ref in refs[:-2])

        own[...] = half(slot)
        away[...] = half(1 - slot).astype(bf16)

    shape = values[0].shape[1:]
    shapes = [jax.ShapeDtypeStruct(shape, f32), jax.ShapeDtypeStruct(shape, bf16)]
    return small_call(kernel, shapes, [], values, "sums")


def kernel_call(kernel, size, slots, tile_rows, name, out_shape, *inputs):
    inside = pl.BlockSpec(memory_space=pltpu.VMEM)
    return pl.pallas_call(
        functools.partial(kernel, size, size // tile_rows, slots, tile_rows),
        out_shape=out_shape,
        in_specs=[inside] * len(inputs),
        out_specs=[inside] * len(out_shape),
        scratch_shapes=[
            pltpu.VMEM((2 * size, size), bf16),
            pltpu.VMEM((size, 2 * size), bf16),
        ],
        compiler_params=pltpu.CompilerParams(vmem_limit_bytes=28 * 1024 * 1024),
        cost_estimate=pl.CostEstimate(
            flops=24 * size**3, bytes_accessed=size * size, transcendentals=0
        ),
        name=name,
    )(*inputs)


def shards(size, object_slab, probe_wave, amplitudes, row_offsets, position_counts):
    tile_rows = object_slab.shape[2]
    span = size // tile_rows
    count = lax.axis_size("tile")
    parts = lax.axis_size("scan")
    slots = amplitudes.shape[0]
    paired = parts == slots == 2
    ahead = span // 2
    swap = [(0, 1), (1, 0)]
    ahead_pairs = [(one, (one + ahead) % count) for one in range(count)]

    def brought(value):
        return lax.ppermute(value, "tile", ahead_pairs)

    def paired_with(value, unit):
        return lax.ppermute(value, "tile", [(one, one ^ unit) for one in range(count)])

    def paired_across(value, unit):
        pairs = []
        for one in range(count):
            step = unit if (one // unit) % 2 else -unit
            pairs.append((one, one + step if unit <= one < count - unit else one ^ 1))
        return lax.ppermute(value, "tile", pairs)

    own = object_slab.astype(bf16)
    width = own.shape[-1]
    if paired:
        beside = lax.ppermute(own, "scan", swap)
        beside, probe_wave = lax.optimization_barrier((beside, probe_wave))
        whole = placed([own, beside], lambda n: jnp.bitwise_xor(lax.axis_index("scan"), n), "halves")
        probe_pieces = [probe_wave, lax.ppermute(probe_wave, "scan", swap)]
        straight, crossed = amplitude_messages(amplitudes, row_offsets, position_counts)
        straight = brought(straight)
        crossed = lax.ppermute(
            crossed,
            ("tile", "scan"),
            [(2 * a + x, 2 * b + 1 - x) for a, b in ahead_pairs for x in range(2)],
        )
        notes = straight
        measured = [straight, crossed]
    else:
        whole = lax.all_gather(own, "scan")
        every = lax.all_gather(probe_wave, "scan")
        probe_pieces = [every[number] for number in range(parts)]
        notes = jnp.concatenate([row_offsets, position_counts]).astype(bf16)
        notes = brought(jnp.pad(notes[None], ((0, 15), (0, size - slots - 1))))
        every = lax.all_gather(brought(amplitudes.astype(bf16)), "scan")
        slot = lax.axis_index("scan")
        measured = [every[:, jnp.minimum(slot, slots - 1)].reshape((size, size))]
    next_across, next_with = paired_across(whole, 4), paired_with(whole, 4)
    near_across, near_with = paired_across(whole, 2), paired_with(whole, 2)
    middle, probe_pieces, notes = lax.optimization_barrier((whole, probe_pieces, notes))
    far_rows, far_cols, near = tables(size)
    turned, far_near, far_far = rolled(
        probe_pieces, far_rows, far_cols, notes, size, span, slots
    )
    arrived = [next_with, near_with, middle, near_across, next_across]
    mine = placed(arrived, group, "groups")
    theirs = paired_with(mine, 1)
    shape = jax.ShapeDtypeStruct
    psi2, field = kernel_call(
        forth_kernel, size, slots, tile_rows, "forth",
        [shape((2, size, size), bf16), shape((2, size, size), f32)],
        notes, mine, theirs, far_cols, near, turned, far_near,
    )
    measured[-1], field = lax.optimization_barrier((measured[-1], field))
    keep, send = kernel_call(
        back_kernel, size, slots, tile_rows, "back",
        [shape((len(arrived), parts, 2, 2, tile_rows, width), bf16)] * 2,
        notes, mine, theirs, far_rows, near, turned, far_far, psi2, field, *measured,
    )
    got = paired_with(send, 1)
    if paired:
        near_with, next_with, next_across, middle, half_own, half_away = merged_in_halves(keep, got)
        half_got = lax.ppermute(half_away, "scan", swap)
        message = summed(half_own, half_got)
        middle, message = lax.optimization_barrier((middle, message))
        kept, away = halves_of_sum(
            [
                paired_with(near_with, 2),
                paired_with(next_with, 4),
                paired_across(next_across, 4),
                middle,
            ]
        )
        for value in (lax.ppermute(away, "scan", swap), paired_across(message, 2)):
            kept = kept + value.astype(f32)
        return kept
    next_with, near_with, middle, near_across, next_across = merged_messages(keep, got)
    returned = [
        paired_with(near_with, 2),
        paired_across(near_across, 2),
        paired_with(next_with, 4),
        paired_across(next_across, 4),
        middle,
    ]
    total = sum(value.astype(f32) for value in returned)
    return lax.psum_scatter(total, "scan", scatter_dimension=0, tiled=False)


def solution(mesh):
    in_specs = (
        P(None, None, "tile", "scan"),
        P(None, None, "scan"),
        P("tile", "scan", None),
        P("tile"),
        P("tile"),
    )
    out_specs = P(None, None, "tile", "scan")

    def run(object_slab, *rest):
        return jax.shard_map(
            functools.partial(shards, object_slab.shape[3]),
            mesh=mesh, in_specs=in_specs, out_specs=out_specs, check_vma=False,
        )(object_slab, *rest)

    return run
```

profile of v0, /device:TPU:0, one launch (start us, length us, event | category | flops | bytes accessed | tf_op | source)
XLA Modules:
  0.0 62.2 jit_solution(12684802293593688544)
XLA Ops:
  0.0 1.0 %convert_element_type.9.refs_0_ = bf16[2,2,64,256]{3,2,1,0:T(8,128)(2,1)S(1)} convert(f32[2,2,64,256]{3,2,1,0:T(8,128)} %param.8) | non-fusion elementwise | flops 65536 | bytes 393216 | tf_op jit(solution)/shard_map/convert_element_type | solution.py:448
  1.0 3.0 %collective-permute-start = (bf16[2,2,64,256]{3,2,1,0:T(8,128)(2,1)S(1)}, bf16[2,2,64,256]{3,2,1,0:T(8,128)(2,1)S(1)}, u32[]{:S(2)}, u32[]{:S(2)}) collective-permute-start(bf16[2,2,64,256]{3,2,1,0:T(8,128)(2,1)S(1)} %convert_element_type.9.refs_0_), channel_id=1, source_target_pairs={{0,1},{1,0},{2,3},{3,2},{4,5},{5,4},{6,7},{7,6},{8,9},{9,8},{10,11... | collective-permute-start | bytes 393224 | tf_op jit(solution)/shard_map/ppermute | solution.py:451
  4.6 1.2 %copy-done = f32[2,256,512]{2,1,0:T(8,128)S(1)} copy-done((f32[2,256,512]{2,1,0:T(8,128)S(1)}, f32[2,256,512]{2,1,0:T(8,128)}, u32[]{:S(2)}) %copy-start) | copy-done | bytes 1048600
  5.9 0.7 %copy-done.1 = s32[2]{0:T(128)S(1)} copy-done((s32[2]{0:T(128)S(1)}, s32[2]{0:T(128)}, u32[]{:S(2)}) %copy-start.1) | copy-done | bytes 32
  6.5 0.6 messages.1
  7.1 1.6 %collective-permute-start.2 = (bf16[272,512]{1,0:T(8,128)(2,1)S(1)}, bf16[272,512]{1,0:T(8,128)(2,1)S(1)}, u32[]{:S(2)}, u32[]{:S(2)}) collective-permute-start(bf16[272,512]{1,0:T(8,128)(2,1)S(1)} %get-tuple-element.34), channel_id=1, source_target_pairs={{0,8},{2,10},{4,12},{6,14},{8,16},{10,18},{12,20},{14,22},{16,24},... | collective-permute-start | bytes 835592 | tf_op jit(solution)/shard_map/ppermute | solution.py:436
  8.7 0.5 collective-permute-start.1
  9.3 0.1 collective-permute-start.6
  9.4 0.5 collective-permute-start.5
  9.9 4.1 %collective-permute-start.4 = (bf16[2,2,2,64,256]{4,3,2,1,0:T(8,128)(2,1)S(1)}, bf16[2,2,2,64,256]{4,3,2,1,0:T(8,128)(2,1)S(1)}, u32[]{:S(2)}, u32[]{:S(2)}) collective-permute-start(bf16[2,2,2,64,256]{4,3,2,1,0:T(8,128)(2,1)S(1)} %halves.1.refs_2_), channel_id=1, source_target_pairs={{0,4},{2,6},{4,0},{6,2},{8,12},{10,14},{12,8},{14,10},{16,20},{18,... | collective-permute-start | bytes 786440 | tf_op jit(solution)/shard_map/ppermute | solution.py:439
  14.0 4.6 %collective-permute-done.2.notes.refs_0_ = bf16[272,512]{1,0:T(8,128)(2,1)S(1)} collective-permute-done((bf16[272,512]{1,0:T(8,128)(2,1)S(1)}, bf16[272,512]{1,0:T(8,128)(2,1)S(1)}, u32[]{:S(2)}, u32[]{:S(2)}) %collective-permute-start.2) | collective-permute-done | bytes 278560 | tf_op jit(solution)/shard_map/ppermute | solution.py:436
  18.6 3.5 %collective-permute-done.1.refs_1_ = bf16[2,512,256]{2,1,0:T(8,128)(2,1)S(1)} collective-permute-done((bf16[2,512,256]{2,1,0:T(8,128)(2,1)}, bf16[2,512,256]{2,1,0:T(8,128)(2,1)S(1)}, u32[]{:S(2)}, u32[]{:S(2)}) %collective-permute-start.1) | collective-permute-done | bytes 524320 | tf_op jit(solution)/shard_map/ppermute | solution.py:454
  22.1 1.7 %collective-permute-done.4.refs_1_ = bf16[2,2,2,64,256]{4,3,2,1,0:T(8,128)(2,1)S(1)} collective-permute-done((bf16[2,2,2,64,256]{4,3,2,1,0:T(8,128)(2,1)S(1)}, bf16[2,2,2,64,256]{4,3,2,1,0:T(8,128)(2,1)S(1)}, u32[]{:S(2)}, u32[]{:S(2)}) %collective-permute-start.4) | collective-permute-done | bytes 262176 | tf_op jit(solution)/shard_map/ppermute | solution.py:439
  23.8 4.7 %collective-permute-done.3.refs_0_ = bf16[2,2,2,64,256]{4,3,2,1,0:T(8,128)(2,1)S(1)} collective-permute-done((bf16[2,2,2,64,256]{4,3,2,1,0:T(8,128)(2,1)S(1)}, bf16[2,2,2,64,256]{4,3,2,1,0:T(8,128)(2,1)S(1)}, u32[]{:S(2)}, u32[]{:S(2)}) %collective-permute-start.3) | collective-permute-done | bytes 262176 | tf_op jit(solution)/shard_map/ppermute | solution.py:439
  28.5 0.1 groups.1.mine
  28.6 0.1 collective-permute-start.7
  28.8 1.4 %rolled.1 = (bf16[2,512,512]{2,1,0:T(8,128)(2,1)S(1)}, bf16[2,512,256]{2,1,0:T(8,128)(2,1)S(1)}, bf16[2,256,512]{2,1,0:T(8,128)(2,1)S(1)}) custom-call(bf16[272,512]{1,0:T(8,128)(2,1)S(1)} %collective-permute-done.2.notes.refs_0_, bf16[2,512,512]{2,1,0:T(8,128)(2,1)S(1)} %copy-done.3, bf16[2,512,512]{2,1,0:T(8,128)(2,1)S(1)} %copy-done.5, ...), custom_call_target="tpu_custom_call" | custom-call | flops 8589934592 | bytes 6291456 | tf_op jit(solution)/shard_map/rolled/pallas_call | solution.py:133
  30.3 1.5 %collective-permute-done.7.theirs = bf16[5,2,2,2,64,256]{5,4,3,2,1,0:T(8,128)(2,1)S(1)} collective-permute-done((bf16[5,2,2,2,64,256]{5,4,3,2,1,0:T(8,128)(2,1)S(1)}, bf16[5,2,2,2,64,256]{5,4,3,2,1,0:T(8,128)(2,1)S(1)}, u32[]{:S(2)}, u32[]{:S(2)}) %collective-permute-start.7) | collective-permute-done | bytes 1310752 | tf_op jit(solution)/shard_map/ppermute | solution.py:439
  31.7 0.1 forth.1
  31.9 8.3 %collective-permute-done.8.refs_1_ = bf16[256,512]{1,0:T(8,128)(2,1)S(1)} collective-permute-done((bf16[256,512]{1,0:T(8,128)(2,1)S(1)}, bf16[256,512]{1,0:T(8,128)(2,1)S(1)}, u32[]{:S(2)}, u32[]{:S(2)}) %collective-permute-start.8) | collective-permute-done | bytes 262176 | tf_op jit(solution)/shard_map/ppermute | solution.py:457
  40.1 0.3 back.1
  40.4 0.1 collective-permute-start.9
  40.5 3.0 %collective-permute-done.9.got = bf16[5,2,2,2,64,256]{5,4,3,2,1,0:T(8,128)(2,1)S(1)} collective-permute-done((bf16[5,2,2,2,64,256]{5,4,3,2,1,0:T(8,128)(2,1)S(1)}, bf16[5,2,2,2,64,256]{5,4,3,2,1,0:T(8,128)(2,1)S(1)}, u32[]{:S(2)}, u32[]{:S(2)}) %collective-permute-start.9) | collective-permute-done | bytes 1310752 | tf_op jit(solution)/shard_map/ppermute | solution.py:439
  43.5 0.3 merge.1
  43.9 5.4 %collective-permute-start.11 = (bf16[2,2,2,64,256]{4,3,2,1,0:T(8,128)(2,1)S(1)}, bf16[2,2,2,64,256]{4,3,2,1,0:T(8,128)(2,1)S(1)}, u32[]{:S(2)}, u32[]{:S(2)}) collective-permute-start(bf16[2,2,2,64,256]{4,3,2,1,0:T(8,128)(2,1)S(1)} %get-tuple-element.50), channel_id=1, source_target_pairs={{0,8},{2,10},{4,12},{6,14},{8,0},{10,2},{12,4},{14,6},{16,24},{18,... | collective-permute-start | bytes 786440 | tf_op jit(solution)/shard_map/ppermute | solution.py:439
  49.3 5.9 %collective-permute-done.13.got = bf16[2,2,64,256]{3,2,1,0:T(8,128)(2,1)S(1)} collective-permute-done((bf16[2,2,64,256]{3,2,1,0:T(8,128)(2,1)S(1)}, bf16[2,2,64,256]{3,2,1,0:T(8,128)(2,1)S(1)}, u32[]{:S(2)}, u32[]{:S(2)}) %collective-permute-start.13) | collective-permute-done | bytes 131104 | tf_op jit(solution)/shard_map/ppermute | solution.py:498
  55.3 0.3 collective-permute-done.11.refs_1_
  55.6 0.1 sums.1
  55.7 0.1 collective-permute-start.14
  55.8 0.8 %collective-permute-done.15 = bf16[2,2,64,256]{3,2,1,0:T(8,128)(2,1)S(1)} collective-permute-done((bf16[2,2,64,256]{3,2,1,0:T(8,128)(2,1)S(1)}, bf16[2,2,64,256]{3,2,1,0:T(8,128)(2,1)S(1)}, u32[]{:S(2)}, u32[]{:S(2)}) %collective-permute-start.15) | collective-permute-done | bytes 131104 | tf_op jit(solution)/shard_map/ppermute | solution.py:446
  56.6 4.8 %collective-permute-done.14 = bf16[2,2,64,256]{3,2,1,0:T(8,128)(2,1)S(1)} collective-permute-done((bf16[2,2,64,256]{3,2,1,0:T(8,128)(2,1)S(1)}, bf16[2,2,64,256]{3,2,1,0:T(8,128)(2,1)S(1)}, u32[]{:S(2)}, u32[]{:S(2)}) %collective-permute-start.14) | collective-permute-done | bytes 131104 | tf_op jit(solution)/shard_map/ppermute | solution.py:509
  61.4 0.7 %convert_add_fusion = f32[2,2,64,256]{3,2,1,0:T(8,128)} fusion(bf16[2,2,64,256]{3,2,1,0:T(8,128)(2,1)S(1)} %collective-permute-done.15, f32[2,2,64,256]{3,2,1,0:T(8,128)S(1)} %get-tuple-element.56, bf16[2,2,64,256]{3,2,1,0:T(8,128)(2,1)S(1)} %collective-permute-done.14), kind=kLoop, calls=%fused_computation | loop fusion | flops 262144 | bytes 786432 | tf_op jit(solution)/shard_map/add | solution.py:510
  (23 shorter events, 0.3 us)
Async XLA Ops:
  1.0 7.8 %collective-permute-start = (bf16[2,2,64,256]{3,2,1,0:T(8,128)(2,1)S(1)}, bf16[2,2,64,256]{3,2,1,0:T(8,128)(2,1)S(1)}, u32[]{:S(2)}, u32[]{:S(2)}) collective-permute-start(bf16[2,2,64,256]{3,2,1,0:T(8,128)(2,1)S(1)} %convert_element_type.9.refs_0_), channel_id=1, source_target_pairs={{0,1},{1,0},{2,3},{3,2},{4,5},{5,4},{6,7},{7,6},{8,9},{9,8},{10,11... | collective-permute-start | bytes 393224 | tf_op jit(solution)/shard_map/ppermute | solution.py:451
  4.6 1.2 %copy-start = (f32[2,256,512]{2,1,0:T(8,128)S(1)}, f32[2,256,512]{2,1,0:T(8,128)}, u32[]{:S(2)}) copy-start(f32[2,256,512]{2,1,0:T(8,128)} %amps.1) | copy-start | bytes 3145732
  5.9 0.7 %copy-start.1 = (s32[2]{0:T(128)S(1)}, s32[2]{0:T(128)}, u32[]{:S(2)}) copy-start(s32[2]{0:T(128)} %offsets.1) | copy-start | bytes 28
  7.1 11.5 %collective-permute-start.2 = (bf16[272,512]{1,0:T(8,128)(2,1)S(1)}, bf16[272,512]{1,0:T(8,128)(2,1)S(1)}, u32[]{:S(2)}, u32[]{:S(2)}) collective-permute-start(bf16[272,512]{1,0:T(8,128)(2,1)S(1)} %get-tuple-element.34), channel_id=1, source_target_pairs={{0,8},{2,10},{4,12},{6,14},{8,16},{10,18},{12,20},{14,22},{16,24},... | collective-permute-start | bytes 835592 | tf_op jit(solution)/shard_map/ppermute | solution.py:436
  8.7 13.3 %collective-permute-start.1 = (bf16[2,512,256]{2,1,0:T(8,128)(2,1)}, bf16[2,512,256]{2,1,0:T(8,128)(2,1)S(1)}, u32[]{:S(2)}, u32[]{:S(2)}) collective-permute-start(bf16[2,512,256]{2,1,0:T(8,128)(2,1)} %refs_0_), channel_id=1, source_target_pairs={{0,1},{1,0},{2,3},{3,2},{4,5},{5,4},{6,7},{7,6},{8,9},{9,8},{10,11... | collective-permute-start | bytes 1572872 | tf_op jit(solution)/shard_map/ppermute | solution.py:454
  9.3 19.5 %copy-start.2 = (bf16[2,512,256]{2,1,0:T(8,128)(2,1)S(1)}, bf16[2,512,256]{2,1,0:T(8,128)(2,1)}, u32[]{:S(2)}) copy-start(bf16[2,512,256]{2,1,0:T(8,128)(2,1)} %refs_0_) | copy-start | bytes 1572868
  9.3 19.5 %copy-start.3 = (bf16[2,512,512]{2,1,0:T(8,128)(2,1)S(1)}, bf16[2,512,512]{2,1,0:T(8,128)(2,1)}, u32[]{:S(2)}) copy-start(bf16[2,512,512]{2,1,0:T(8,128)(2,1)} %constant.6.clone.far_rows) | copy-start | bytes 3145732
  9.3 19.5 %copy-start.5 = (bf16[2,512,512]{2,1,0:T(8,128)(2,1)S(1)}, bf16[2,512,512]{2,1,0:T(8,128)(2,1)}, u32[]{:S(2)}) copy-start(bf16[2,512,512]{2,1,0:T(8,128)(2,1)} %constant.7.clone.far_cols) | copy-start | bytes 3145732
  9.3 12.7 %collective-permute-start.6 = (bf16[2,2,2,64,256]{4,3,2,1,0:T(8,128)(2,1)S(1)}, bf16[2,2,2,64,256]{4,3,2,1,0:T(8,128)(2,1)S(1)}, u32[]{:S(2)}, u32[]{:S(2)}) collective-permute-start(bf16[2,2,2,64,256]{4,3,2,1,0:T(8,128)(2,1)S(1)} %halves.1.refs_2_), channel_id=1, source_target_pairs={{0,2},{2,0},{4,6},{6,4},{8,16},{10,18},{12,20},{14,22},{16,8},{18,... | collective-permute-start | bytes 786440 | tf_op jit(solution)/shard_map/ppermute | solution.py:446
  9.4 12.6 %collective-permute-start.5 = (bf16[2,2,2,64,256]{4,3,2,1,0:T(8,128)(2,1)S(1)}, bf16[2,2,2,64,256]{4,3,2,1,0:T(8,128)(2,1)S(1)}, u32[]{:S(2)}, u32[]{:S(2)}) collective-permute-start(bf16[2,2,2,64,256]{4,3,2,1,0:T(8,128)(2,1)S(1)} %halves.1.refs_2_), channel_id=1, source_target_pairs={{0,2},{2,0},{4,8},{6,10},{8,4},{10,6},{12,16},{14,18},{16,12},{18,... | collective-permute-start | bytes 786440 | tf_op jit(solution)/shard_map/ppermute | solution.py:446
  9.9 13.9 %collective-permute-start.4 = (bf16[2,2,2,64,256]{4,3,2,1,0:T(8,128)(2,1)S(1)}, bf16[2,2,2,64,256]{4,3,2,1,0:T(8,128)(2,1)S(1)}, u32[]{:S(2)}, u32[]{:S(2)}) collective-permute-start(bf16[2,2,2,64,256]{4,3,2,1,0:T(8,128)(2,1)S(1)} %halves.1.refs_2_), channel_id=1, source_target_pairs={{0,4},{2,6},{4,0},{6,2},{8,12},{10,14},{12,8},{14,10},{16,20},{18,... | collective-permute-start | bytes 786440 | tf_op jit(solution)/shard_map/ppermute | solution.py:439
  18.6 9.9 %collective-permute-start.3 = (bf16[2,2,2,64,256]{4,3,2,1,0:T(8,128)(2,1)S(1)}, bf16[2,2,2,64,256]{4,3,2,1,0:T(8,128)(2,1)S(1)}, u32[]{:S(2)}, u32[]{:S(2)}) collective-permute-start(bf16[2,2,2,64,256]{4,3,2,1,0:T(8,128)(2,1)S(1)} %halves.1.refs_2_), channel_id=1, source_target_pairs={{0,8},{2,10},{4,12},{6,14},{8,0},{10,2},{12,4},{14,6},{16,24},{18,... | collective-permute-start | bytes 786440 | tf_op jit(solution)/shard_map/ppermute | solution.py:439
  28.6 3.1 %collective-permute-start.7 = (bf16[5,2,2,2,64,256]{5,4,3,2,1,0:T(8,128)(2,1)S(1)}, bf16[5,2,2,2,64,256]{5,4,3,2,1,0:T(8,128)(2,1)S(1)}, u32[]{:S(2)}, u32[]{:S(2)}) collective-permute-start(bf16[5,2,2,2,64,256]{5,4,3,2,1,0:T(8,128)(2,1)S(1)} %groups.1.mine), channel_id=1, source_target_pairs={{0,2},{2,0},{4,6},{6,4},{8,10},{10,8},{12,14},{14,12},{16,18},{18,... | collective-permute-start | bytes 3932168 | tf_op jit(solution)/shard_map/ppermute | solution.py:439
  28.8 3.0 %copy-start.4 = (bf16[2,512,512]{2,1,0:T(8,128)(2,1)S(1)}, bf16[2,512,512]{2,1,0:T(8,128)(2,1)}, u32[]{:S(2)}) copy-start(bf16[2,512,512]{2,1,0:T(8,128)(2,1)} %constant.8.clone.near) | copy-start | bytes 3145732
  28.8 11.4 %collective-permute-start.8 = (bf16[256,512]{1,0:T(8,128)(2,1)S(1)}, bf16[256,512]{1,0:T(8,128)(2,1)S(1)}, u32[]{:S(2)}, u32[]{:S(2)}) collective-permute-start(bf16[256,512]{1,0:T(8,128)(2,1)S(1)} %get-tuple-element.43), channel_id=1, source_target_pairs={{0,9},{1,8},{2,11},{3,10},{4,13},{5,12},{6,15},{7,14},{8,17},{9,16... | collective-permute-start | bytes 786440 | tf_op jit(solution)/shard_map/ppermute | solution.py:457
  40.4 3.1 %collective-permute-start.9 = (bf16[5,2,2,2,64,256]{5,4,3,2,1,0:T(8,128)(2,1)S(1)}, bf16[5,2,2,2,64,256]{5,4,3,2,1,0:T(8,128)(2,1)S(1)}, u32[]{:S(2)}, u32[]{:S(2)}) collective-permute-start(bf16[5,2,2,2,64,256]{5,4,3,2,1,0:T(8,128)(2,1)S(1)} %get-tuple-element.48), channel_id=1, source_target_pairs={{0,2},{2,0},{4,6},{6,4},{8,10},{10,8},{12,14},{14,12},{16,18},{18,... | collective-permute-start | bytes 3932168 | tf_op jit(solution)/shard_map/ppermute | solution.py:439
  43.8 11.5 %collective-permute-start.10 = (bf16[2,2,2,64,256]{4,3,2,1,0:T(8,128)(2,1)S(1)}, bf16[2,2,2,64,256]{4,3,2,1,0:T(8,128)(2,1)S(1)}, u32[]{:S(2)}, u32[]{:S(2)}) collective-permute-start(bf16[2,2,2,64,256]{4,3,2,1,0:T(8,128)(2,1)S(1)} %get-tuple-element.49), channel_id=1, source_target_pairs={{0,4},{2,6},{4,0},{6,2},{8,12},{10,14},{12,8},{14,10},{16,20},{18,... | collective-permute-start | bytes 786440 | tf_op jit(solution)/shard_map/ppermute | solution.py:439
  43.9 11.7 %collective-permute-start.11 = (bf16[2,2,2,64,256]{4,3,2,1,0:T(8,128)(2,1)S(1)}, bf16[2,2,2,64,256]{4,3,2,1,0:T(8,128)(2,1)S(1)}, u32[]{:S(2)}, u32[]{:S(2)}) collective-permute-start(bf16[2,2,2,64,256]{4,3,2,1,0:T(8,128)(2,1)S(1)} %get-tuple-element.50), channel_id=1, source_target_pairs={{0,8},{2,10},{4,12},{6,14},{8,0},{10,2},{12,4},{14,6},{16,24},{18,... | collective-permute-start | bytes 786440 | tf_op jit(solution)/shard_map/ppermute | solution.py:439
  49.3 6.3 %collective-permute-start.12 = (bf16[2,2,2,64,256]{4,3,2,1,0:T(8,128)(2,1)S(1)}, bf16[2,2,2,64,256]{4,3,2,1,0:T(8,128)(2,1)S(1)}, u32[]{:S(2)}, u32[]{:S(2)}) collective-permute-start(bf16[2,2,2,64,256]{4,3,2,1,0:T(8,128)(2,1)S(1)} %get-tuple-element.51), channel_id=1, source_target_pairs={{0,2},{2,0},{4,6},{6,4},{8,16},{10,18},{12,20},{14,22},{16,8},{18,... | collective-permute-start | bytes 786440 | tf_op jit(solution)/shard_map/ppermute | solution.py:446
  49.3 5.9 %collective-permute-start.13 = (bf16[2,2,64,256]{3,2,1,0:T(8,128)(2,1)S(1)}, bf16[2,2,64,256]{3,2,1,0:T(8,128)(2,1)S(1)}, u32[]{:S(2)}, u32[]{:S(2)}) collective-permute-start(bf16[2,2,64,256]{3,2,1,0:T(8,128)(2,1)S(1)} %get-tuple-element.54), channel_id=1, source_target_pairs={{0,1},{1,0},{2,3},{3,2},{4,5},{5,4},{6,7},{7,6},{8,9},{9,8},{10,11... | collective-permute-start | bytes 393224 | tf_op jit(solution)/shard_map/ppermute | solution.py:498
  55.2 1.4 %collective-permute-start.15 = (bf16[2,2,64,256]{3,2,1,0:T(8,128)(2,1)S(1)}, bf16[2,2,64,256]{3,2,1,0:T(8,128)(2,1)S(1)}, u32[]{:S(2)}, u32[]{:S(2)}) collective-permute-start(bf16[2,2,64,256]{3,2,1,0:T(8,128)(2,1)S(1)} %near.3), channel_id=1, source_target_pairs={{0,2},{2,0},{4,8},{6,10},{8,4},{10,6},{12,16},{14,18},{16,12},{18,... | collective-permute-start | bytes 393224 | tf_op jit(solution)/shard_map/ppermute | solution.py:446
  55.7 5.7 %collective-permute-start.14 = (bf16[2,2,64,256]{3,2,1,0:T(8,128)(2,1)S(1)}, bf16[2,2,64,256]{3,2,1,0:T(8,128)(2,1)S(1)}, u32[]{:S(2)}, u32[]{:S(2)}) collective-permute-start(bf16[2,2,64,256]{3,2,1,0:T(8,128)(2,1)S(1)} %get-tuple-element.57), channel_id=1, source_target_pairs={{0,1},{1,0},{2,3},{3,2},{4,5},{5,4},{6,7},{7,6},{8,9},{9,8},{10,11... | collective-permute-start | bytes 393224 | tf_op jit(solution)/shard_map/ppermute | solution.py:509
where the time goes:
time: 62.4 us; the launch traced here: 62.2 us
  waiting for transfers between devices  39 us (62%)
  starting transfers between devices  15.7 us (25%)
  Pallas kernels  3.04 us (5%)
  local copies, waits for them, and re-layouts  1.9 us (3%)
  other arithmetic  1.7 us (3%)
  between operations  0.82 us (1%)
    ppermute x6, waiting for transfers between devices, paired_with(): lax.ppermute(value, 'tile', [(one, one ^ unit) for one in range(count)])  11.2 us
    ppermute x6, starting transfers between devices, paired_with(): lax.ppermute(value, 'tile', [(one, one ^ unit) for one in range(count)])  9.73 us
    ppermute x1, waiting for transfers between devices, shards(): lax.ppermute(crossed, ('tile', 'scan'), [(2 * a + x, 2 * b + 1 - x) for a...  8.26 us
    ppermute x1, waiting for transfers between devices, shards(): half_got = lax.ppermute(half_away, 'scan', swap)  5.91 us
    ppermute x1, waiting for transfers between devices, shards(): lax.ppermute(away, 'scan', swap)  4.78 us
    ppermute x1, waiting for transfers between devices, brought(): return lax.ppermute(value, 'tile', ahead_pairs)  4.56 us
    ppermute x1, waiting for transfers between devices, shards(): probe_pieces = [probe_wave, lax.ppermute(probe_wave, 'scan', swap)]  3.47 us
    ppermute x1, starting transfers between devices, shards(): beside = lax.ppermute(own, 'scan', swap)  3 us
  transfers between devices with their start and end apart: 16, of which 11 were waited for; matrix products, arithmetic and copies ran while one was open for 0% of the time, Pallas kernels for 4%

commit v1 on v0

--- a/solution.py
+++ b/solution.py
@@ -331,6 +331,18 @@
     return small_call(kernel, shape, [], values, name)
 
 
+def placed_groups(next_with, near_with, middle, next_across, own_half, other_half):
+    def kernel(*refs):
+        out, slot = refs[-1], lax.axis_index("scan")
+        for number, value in zip((0, 1, 2, 4), refs[:4]):
+            out[group(number)] = value[...]
+        out[group(3), slot] = refs[4][...]
+        out[group(3), 1 - slot] = refs[5][...]
+
+    values = [next_with, near_with, middle, next_across, own_half, other_half]
+    return small_call(kernel, jax.ShapeDtypeStruct((5,) + middle.shape, bf16), [], values, "groups")
+
+
 def amplitude_messages(amplitudes, row_offsets, position_counts):
     slots, rows, size = amplitudes.shape
 
@@ -449,10 +461,12 @@
     width = own.shape[-1]
     if paired:
         beside = lax.ppermute(own, "scan", swap)
-        beside, probe_wave = lax.optimization_barrier((beside, probe_wave))
+        straight, crossed = amplitude_messages(amplitudes, row_offsets, position_counts)
+        beside, probe_wave, own_late, straight = lax.optimization_barrier(
+            (beside, probe_wave, own, straight)
+        )
         whole = placed([own, beside], lambda n: jnp.bitwise_xor(lax.axis_index("scan"), n), "halves")
         probe_pieces = [probe_wave, lax.ppermute(probe_wave, "scan", swap)]
-        straight, crossed = amplitude_messages(amplitudes, row_offsets, position_counts)
         straight = brought(straight)
         crossed = lax.ppermute(
             crossed,
@@ -471,14 +485,21 @@
         slot = lax.axis_index("scan")
         measured = [every[:, jnp.minimum(slot, slots - 1)].reshape((size, size))]
     next_across, next_with = paired_across(whole, 4), paired_with(whole, 4)
-    near_across, near_with = paired_across(whole, 2), paired_with(whole, 2)
+    near_with = paired_with(whole, 2)
+    near_across = paired_across(own_late if paired else whole, 2)
+    if paired:
+        near_beside = lax.ppermute(near_across, "scan", swap)
     middle, probe_pieces, notes = lax.optimization_barrier((whole, probe_pieces, notes))
     far_rows, far_cols, near = tables(size)
     turned, far_near, far_far = rolled(
         probe_pieces, far_rows, far_cols, notes, size, span, slots
     )
-    arrived = [next_with, near_with, middle, near_across, next_across]
-    mine = placed(arrived, group, "groups")
+    if paired:
+        mine = placed_groups(
+            next_with, near_with, middle, next_across, near_across, near_beside
+        )
+    else:
+        mine = placed([next_with, near_with, middle, near_across, next_across], group, "groups")
     theirs = paired_with(mine, 1)
     shape = jax.ShapeDtypeStruct
     psi2, field = kernel_call(
@@ -489,7 +510,7 @@
     measured[-1], field = lax.optimization_barrier((measured[-1], field))
     keep, send = kernel_call(
         back_kernel, size, slots, tile_rows, "back",
-        [shape((len(arrived), parts, 2, 2, tile_rows, width), bf16)] * 2,
+        [shape((5, parts, 2, 2, tile_rows, width), bf16)] * 2,
         notes, mine, theirs, far_rows, near, turned, far_far, psi2, field, *measured,
     )
     got = paired_with(send, 1)

time: 62.4 us -> 63.3 us (1.014)
  starting transfers between devices: 15.7 us -> 29.1 us
  waiting for transfers between devices: 39 us -> 26.5 us
    ppermute x6, starting transfers between devices: 9.73 us -> 18.3 us  [paired_with(): lax.ppermute(value, 'tile', [(one, one ^ unit) for one in range(count)])]
    ppermute x6, waiting for transfers between devices: 11.2 us -> 3.64 us  [paired_with(): lax.ppermute(value, 'tile', [(one, one ^ unit) for one in range(count)])]
    ppermute x1, waiting for transfers between devices: 4.56 us -> 0.01 us  [brought(): return lax.ppermute(value, 'tile', ahead_pairs)]
    ppermute x0 -> x1, waiting for transfers between devices: none -> 4.37 us  [shards(): near_beside = lax.ppermute(near_across, 'scan', swap)]
    ppermute x1, waiting for transfers between devices: 3.47 us -> 0.01 us  [shards(): probe_pieces = [probe_wave, lax.ppermute(probe_wave, 'scan', swap)]]
    ppermute x1, starting transfers between devices: 0.03 us -> 1.83 us  [shards(): lax.ppermute(crossed, ('tile', 'scan'), [(2 * a + x, 2 * b + 1 - x) for a...]
    ppermute x1, starting transfers between devices: 0.54 us -> 1.74 us  [shards(): probe_pieces = [probe_wave, lax.ppermute(probe_wave, 'scan', swap)]]
    ppermute x1, starting transfers between devices: 0.01 us -> 0.66 us  [shards(): half_got = lax.ppermute(half_away, 'scan', swap)]
  transfers between devices with their start and end apart: 16 -> 17, of which waited for: 11 -> 9; matrix products, arithmetic and copies ran while one was open for 0% -> 0% of each run, Pallas kernels for 4% -> 4%
where the time goes in v1:
time: 63.3 us; the launch traced here: 63.1 us
  starting transfers between devices  29.1 us (46%)
  waiting for transfers between devices  26.5 us (42%)
  Pallas kernels  3.04 us (5%)
  local copies, waits for them, and re-layouts  1.9 us (3%)
  other arithmetic  1.7 us (3%)
  between operations  0.81 us (1%)
    ppermute x6, starting transfers between devices, paired_with(): lax.ppermute(value, 'tile', [(one, one ^ unit) for one in range(count)])  18.3 us
    ppermute x1, waiting for transfers between devices, shards(): lax.ppermute(crossed, ('tile', 'scan'), [(2 * a + x, 2 * b + 1 - x) for a...  7.97 us
    ppermute x1, waiting for transfers between devices, shards(): half_got = lax.ppermute(half_away, 'scan', swap)  5.25 us
    ppermute x1, waiting for transfers between devices, shards(): lax.ppermute(away, 'scan', swap)  4.78 us
    ppermute x1, waiting for transfers between devices, shards(): near_beside = lax.ppermute(near_across, 'scan', swap)  4.37 us
    ppermute x6, waiting for transfers between devices, paired_with(): lax.ppermute(value, 'tile', [(one, one ^ unit) for one in range(count)])  3.64 us
    ppermute x1, starting transfers between devices, shards(): beside = lax.ppermute(own, 'scan', swap)  3 us
    unnamed x12, local copies, waits for them, and re-layouts  1.9 us
  transfers between devices with their start and end apart: 17, of which 9 were waited for; matrix products, arithmetic and copies ran while one was open for 0% of the time, Pallas kernels for 4%

profile of v1, /device:TPU:0, one launch (start us, length us, event | category | flops | bytes accessed | tf_op | source)
XLA Modules:
  0.0 63.1 jit_solution(11872871429775035189)
XLA Ops:
  0.0 1.0 %convert_element_type.9.refs_0_ = bf16[2,2,64,256]{3,2,1,0:T(8,128)(2,1)S(1)} convert(f32[2,2,64,256]{3,2,1,0:T(8,128)} %param.8) | non-fusion elementwise | flops 65536 | bytes 393216 | tf_op jit(solution)/shard_map/convert_element_type | solution.py:460
  1.0 3.0 %collective-permute-start = (bf16[2,2,64,256]{3,2,1,0:T(8,128)(2,1)S(1)}, bf16[2,2,64,256]{3,2,1,0:T(8,128)(2,1)S(1)}, u32[]{:S(2)}, u32[]{:S(2)}) collective-permute-start(bf16[2,2,64,256]{3,2,1,0:T(8,128)(2,1)S(1)} %convert_element_type.9.refs_0_), channel_id=1, source_target_pairs={{0,1},{1,0},{2,3},{3,2},{4,5},{5,4},{6,7},{7,6},{8,9},{9,8},{10,11... | collective-permute-start | bytes 393224 | tf_op jit(solution)/shard_map/ppermute | solution.py:463
  4.6 1.2 %copy-done = f32[2,256,512]{2,1,0:T(8,128)S(1)} copy-done((f32[2,256,512]{2,1,0:T(8,128)S(1)}, f32[2,256,512]{2,1,0:T(8,128)}, u32[]{:S(2)}) %copy-start) | copy-done | bytes 1048600
  5.9 0.7 %copy-done.1 = s32[2]{0:T(128)S(1)} copy-done((s32[2]{0:T(128)S(1)}, s32[2]{0:T(128)}, u32[]{:S(2)}) %copy-start.1) | copy-done | bytes 32
  6.5 0.6 messages.1
  7.1 0.4 collective-permute-done.refs_1_
  7.5 1.7 %collective-permute-start.1 = (bf16[2,512,256]{2,1,0:T(8,128)(2,1)}, bf16[2,512,256]{2,1,0:T(8,128)(2,1)S(1)}, u32[]{:S(2)}, u32[]{:S(2)}) collective-permute-start(bf16[2,512,256]{2,1,0:T(8,128)(2,1)} %refs_0_), channel_id=1, source_target_pairs={{0,1},{1,0},{2,3},{3,2},{4,5},{5,4},{6,7},{7,6},{8,9},{9,8},{10,11... | collective-permute-start | bytes 1572872 | tf_op jit(solution)/shard_map/ppermute | solution.py:469
  9.2 1.6 %collective-permute-start.2 = (bf16[272,512]{1,0:T(8,128)(2,1)S(1)}, bf16[272,512]{1,0:T(8,128)(2,1)S(1)}, u32[]{:S(2)}, u32[]{:S(2)}) collective-permute-start(bf16[272,512]{1,0:T(8,128)(2,1)S(1)} %get-tuple-element.37), channel_id=1, source_target_pairs={{0,8},{2,10},{4,12},{6,14},{8,16},{10,18},{12,20},{14,22},{16,24},... | collective-permute-start | bytes 835592 | tf_op jit(solution)/shard_map/ppermute | solution.py:448
  10.9 0.6 collective-permute-start.5
  11.4 2.6 %collective-permute-start.4 = (bf16[2,2,2,64,256]{4,3,2,1,0:T(8,128)(2,1)S(1)}, bf16[2,2,2,64,256]{4,3,2,1,0:T(8,128)(2,1)S(1)}, u32[]{:S(2)}, u32[]{:S(2)}) collective-permute-start(bf16[2,2,2,64,256]{4,3,2,1,0:T(8,128)(2,1)S(1)} %halves.1.refs_2_), channel_id=1, source_target_pairs={{0,4},{2,6},{4,0},{6,2},{8,12},{10,14},{12,8},{14,10},{16,20},{18,... | collective-permute-start | bytes 786440 | tf_op jit(solution)/shard_map/ppermute | solution.py:451
  14.0 7.9 %collective-permute-start.3 = (bf16[2,2,2,64,256]{4,3,2,1,0:T(8,128)(2,1)S(1)}, bf16[2,2,2,64,256]{4,3,2,1,0:T(8,128)(2,1)S(1)}, u32[]{:S(2)}, u32[]{:S(2)}) collective-permute-start(bf16[2,2,2,64,256]{4,3,2,1,0:T(8,128)(2,1)S(1)} %halves.1.refs_2_), channel_id=1, source_target_pairs={{0,8},{2,10},{4,12},{6,14},{8,0},{10,2},{12,4},{14,6},{16,24},{18,... | collective-permute-start | bytes 786440 | tf_op jit(solution)/shard_map/ppermute | solution.py:451
  21.9 0.6 collective-permute-start.7
  22.5 4.4 %collective-permute-done.7.refs_5_ = bf16[2,2,64,256]{3,2,1,0:T(8,128)(2,1)S(1)} collective-permute-done((bf16[2,2,64,256]{3,2,1,0:T(8,128)(2,1)S(1)}, bf16[2,2,64,256]{3,2,1,0:T(8,128)(2,1)S(1)}, u32[]{:S(2)}, u32[]{:S(2)}) %collective-permute-start.7) | collective-permute-done | bytes 131104 | tf_op jit(solution)/shard_map/ppermute | solution.py:491
  26.9 0.3 collective-permute-done.3.refs_0_
  27.2 0.1 groups.1.mine
  27.4 1.8 %collective-permute-start.9 = (bf16[256,512]{1,0:T(8,128)(2,1)S(1)}, bf16[256,512]{1,0:T(8,128)(2,1)S(1)}, u32[]{:S(2)}, u32[]{:S(2)}) collective-permute-start(bf16[256,512]{1,0:T(8,128)(2,1)S(1)} %get-tuple-element.47), channel_id=1, source_target_pairs={{0,9},{1,8},{2,11},{3,10},{4,13},{5,12},{6,15},{7,14},{8,17},{9,16... | collective-permute-start | bytes 786440 | tf_op jit(solution)/shard_map/ppermute | solution.py:471
  29.2 1.4 %rolled.1 = (bf16[2,512,512]{2,1,0:T(8,128)(2,1)S(1)}, bf16[2,512,256]{2,1,0:T(8,128)(2,1)S(1)}, bf16[2,256,512]{2,1,0:T(8,128)(2,1)S(1)}) custom-call(bf16[272,512]{1,0:T(8,128)(2,1)S(1)} %collective-permute-done.2.notes.refs_0_, bf16[2,512,512]{2,1,0:T(8,128)(2,1)S(1)} %copy-done.3, bf16[2,512,512]{2,1,0:T(8,128)(2,1)S(1)} %copy-done.5, ...), custom_call_target="tpu_custom_call" | custom-call | flops 8589934592 | bytes 6291456 | tf_op jit(solution)/shard_map/rolled/pallas_call | solution.py:133
  30.7 0.1 forth.1
  30.8 8.0 %collective-permute-done.9.refs_1_ = bf16[256,512]{1,0:T(8,128)(2,1)S(1)} collective-permute-done((bf16[256,512]{1,0:T(8,128)(2,1)S(1)}, bf16[256,512]{1,0:T(8,128)(2,1)S(1)}, u32[]{:S(2)}, u32[]{:S(2)}) %collective-permute-start.9) | collective-permute-done | bytes 262176 | tf_op jit(solution)/shard_map/ppermute | solution.py:471
  38.8 0.3 back.1
  39.2 3.0 %collective-permute-done.10.got = bf16[5,2,2,2,64,256]{5,4,3,2,1,0:T(8,128)(2,1)S(1)} collective-permute-done((bf16[5,2,2,2,64,256]{5,4,3,2,1,0:T(8,128)(2,1)S(1)}, bf16[5,2,2,2,64,256]{5,4,3,2,1,0:T(8,128)(2,1)S(1)}, u32[]{:S(2)}, u32[]{:S(2)}) %collective-permute-start.10) | collective-permute-done | bytes 1310752 | tf_op jit(solution)/shard_map/ppermute | solution.py:451
  42.2 0.3 merge.1
  42.5 3.7 %collective-permute-start.11 = (bf16[2,2,2,64,256]{4,3,2,1,0:T(8,128)(2,1)S(1)}, bf16[2,2,2,64,256]{4,3,2,1,0:T(8,128)(2,1)S(1)}, u32[]{:S(2)}, u32[]{:S(2)}) collective-permute-start(bf16[2,2,2,64,256]{4,3,2,1,0:T(8,128)(2,1)S(1)} %get-tuple-element.53), channel_id=1, source_target_pairs={{0,4},{2,6},{4,0},{6,2},{8,12},{10,14},{12,8},{14,10},{16,20},{18,... | collective-permute-start | bytes 786440 | tf_op jit(solution)/shard_map/ppermute | solution.py:451
  46.2 4.0 %collective-permute-start.12 = (bf16[2,2,2,64,256]{4,3,2,1,0:T(8,128)(2,1)S(1)}, bf16[2,2,2,64,256]{4,3,2,1,0:T(8,128)(2,1)S(1)}, u32[]{:S(2)}, u32[]{:S(2)}) collective-permute-start(bf16[2,2,2,64,256]{4,3,2,1,0:T(8,128)(2,1)S(1)} %get-tuple-element.54), channel_id=1, source_target_pairs={{0,8},{2,10},{4,12},{6,14},{8,0},{10,2},{12,4},{14,6},{16,24},{18,... | collective-permute-start | bytes 786440 | tf_op jit(solution)/shard_map/ppermute | solution.py:451
  50.2 0.7 %collective-permute-start.14 = (bf16[2,2,64,256]{3,2,1,0:T(8,128)(2,1)S(1)}, bf16[2,2,64,256]{3,2,1,0:T(8,128)(2,1)S(1)}, u32[]{:S(2)}, u32[]{:S(2)}) collective-permute-start(bf16[2,2,64,256]{3,2,1,0:T(8,128)(2,1)S(1)} %get-tuple-element.58), channel_id=1, source_target_pairs={{0,1},{1,0},{2,3},{3,2},{4,5},{5,4},{6,7},{7,6},{8,9},{9,8},{10,11... | collective-permute-start | bytes 393224 | tf_op jit(solution)/shard_map/ppermute | solution.py:519
  50.9 5.2 %collective-permute-done.14.got = bf16[2,2,64,256]{3,2,1,0:T(8,128)(2,1)S(1)} collective-permute-done((bf16[2,2,64,256]{3,2,1,0:T(8,128)(2,1)S(1)}, bf16[2,2,64,256]{3,2,1,0:T(8,128)(2,1)S(1)}, u32[]{:S(2)}, u32[]{:S(2)}) %collective-permute-start.14) | collective-permute-done | bytes 131104 | tf_op jit(solution)/shard_map/ppermute | solution.py:519
  56.3 0.3 collective-permute-done.12.refs_1_
  56.6 0.1 sums.1
  56.7 0.7 %collective-permute-start.15 = (bf16[2,2,64,256]{3,2,1,0:T(8,128)(2,1)S(1)}, bf16[2,2,64,256]{3,2,1,0:T(8,128)(2,1)S(1)}, u32[]{:S(2)}, u32[]{:S(2)}) collective-permute-start(bf16[2,2,64,256]{3,2,1,0:T(8,128)(2,1)S(1)} %get-tuple-element.61), channel_id=1, source_target_pairs={{0,1},{1,0},{2,3},{3,2},{4,5},{5,4},{6,7},{7,6},{8,9},{9,8},{10,11... | collective-permute-start | bytes 393224 | tf_op jit(solution)/shard_map/ppermute | solution.py:530
  57.4 0.2 collective-permute-done.16
  57.6 4.8 %collective-permute-done.15 = bf16[2,2,64,256]{3,2,1,0:T(8,128)(2,1)S(1)} collective-permute-done((bf16[2,2,64,256]{3,2,1,0:T(8,128)(2,1)S(1)}, bf16[2,2,64,256]{3,2,1,0:T(8,128)(2,1)S(1)}, u32[]{:S(2)}, u32[]{:S(2)}) %collective-permute-start.15) | collective-permute-done | bytes 131104 | tf_op jit(solution)/shard_map/ppermute | solution.py:530
  62.4 0.7 %convert_add_fusion = f32[2,2,64,256]{3,2,1,0:T(8,128)} fusion(bf16[2,2,64,256]{3,2,1,0:T(8,128)(2,1)S(1)} %collective-permute-done.16, f32[2,2,64,256]{3,2,1,0:T(8,128)S(1)} %get-tuple-element.60, bf16[2,2,64,256]{3,2,1,0:T(8,128)(2,1)S(1)} %collective-permute-done.15), kind=kLoop, calls=%fused_computation | loop fusion | flops 262144 | bytes 786432 | tf_op jit(solution)/shard_map/add | solution.py:531
  (25 shorter events, 0.3 us)
Async XLA Ops:
  1.0 6.5 %collective-permute-start = (bf16[2,2,64,256]{3,2,1,0:T(8,128)(2,1)S(1)}, bf16[2,2,64,256]{3,2,1,0:T(8,128)(2,1)S(1)}, u32[]{:S(2)}, u32[]{:S(2)}) collective-permute-start(bf16[2,2,64,256]{3,2,1,0:T(8,128)(2,1)S(1)} %convert_element_type.9.refs_0_), channel_id=1, source_target_pairs={{0,1},{1,0},{2,3},{3,2},{4,5},{5,4},{6,7},{7,6},{8,9},{9,8},{10,11... | collective-permute-start | bytes 393224 | tf_op jit(solution)/shard_map/ppermute | solution.py:463
  4.6 1.2 %copy-start = (f32[2,256,512]{2,1,0:T(8,128)S(1)}, f32[2,256,512]{2,1,0:T(8,128)}, u32[]{:S(2)}) copy-start(f32[2,256,512]{2,1,0:T(8,128)} %amps.1) | copy-start | bytes 3145732
  5.9 0.7 %copy-start.1 = (s32[2]{0:T(128)S(1)}, s32[2]{0:T(128)}, u32[]{:S(2)}) copy-start(s32[2]{0:T(128)} %offsets.1) | copy-start | bytes 28
  7.5 15.0 %collective-permute-start.1 = (bf16[2,512,256]{2,1,0:T(8,128)(2,1)}, bf16[2,512,256]{2,1,0:T(8,128)(2,1)S(1)}, u32[]{:S(2)}, u32[]{:S(2)}) collective-permute-start(bf16[2,512,256]{2,1,0:T(8,128)(2,1)} %refs_0_), channel_id=1, source_target_pairs={{0,1},{1,0},{2,3},{3,2},{4,5},{5,4},{6,7},{7,6},{8,9},{9,8},{10,11... | collective-permute-start | bytes 1572872 | tf_op jit(solution)/shard_map/ppermute | solution.py:469
  9.2 12.7 %collective-permute-start.2 = (bf16[272,512]{1,0:T(8,128)(2,1)S(1)}, bf16[272,512]{1,0:T(8,128)(2,1)S(1)}, u32[]{:S(2)}, u32[]{:S(2)}) collective-permute-start(bf16[272,512]{1,0:T(8,128)(2,1)S(1)} %get-tuple-element.37), channel_id=1, source_target_pairs={{0,8},{2,10},{4,12},{6,14},{8,16},{10,18},{12,20},{14,22},{16,24},... | collective-permute-start | bytes 835592 | tf_op jit(solution)/shard_map/ppermute | solution.py:448
  10.8 3.3 %collective-permute-start.6 = (bf16[2,2,64,256]{3,2,1,0:T(8,128)(2,1)S(1)}, bf16[2,2,64,256]{3,2,1,0:T(8,128)(2,1)S(1)}, u32[]{:S(2)}, u32[]{:S(2)}) collective-permute-start(bf16[2,2,64,256]{3,2,1,0:T(8,128)(2,1)S(1)} %convert_element_type.9.refs_0_), channel_id=1, source_target_pairs={{0,2},{2,0},{4,8},{6,10},{8,4},{10,6},{12,16},{14,18},{16,12},{18,... | collective-permute-start | bytes 393224 | tf_op jit(solution)/shard_map/ppermute | solution.py:458
  10.8 18.4 %copy-start.2 = (bf16[2,512,256]{2,1,0:T(8,128)(2,1)S(1)}, bf16[2,512,256]{2,1,0:T(8,128)(2,1)}, u32[]{:S(2)}) copy-start(bf16[2,512,256]{2,1,0:T(8,128)(2,1)} %refs_0_) | copy-start | bytes 1572868
  10.8 18.4 %copy-start.3 = (bf16[2,512,512]{2,1,0:T(8,128)(2,1)S(1)}, bf16[2,512,512]{2,1,0:T(8,128)(2,1)}, u32[]{:S(2)}) copy-start(bf16[2,512,512]{2,1,0:T(8,128)(2,1)} %constant.6.clone.far_rows) | copy-start | bytes 3145732
  10.8 18.4 %copy-start.5 = (bf16[2,512,512]{2,1,0:T(8,128)(2,1)S(1)}, bf16[2,512,512]{2,1,0:T(8,128)(2,1)}, u32[]{:S(2)}) copy-start(bf16[2,512,512]{2,1,0:T(8,128)(2,1)} %constant.7.clone.far_cols) | copy-start | bytes 3145732
  10.9 16.0 %collective-permute-start.5 = (bf16[2,2,2,64,256]{4,3,2,1,0:T(8,128)(2,1)S(1)}, bf16[2,2,2,64,256]{4,3,2,1,0:T(8,128)(2,1)S(1)}, u32[]{:S(2)}, u32[]{:S(2)}) collective-permute-start(bf16[2,2,2,64,256]{4,3,2,1,0:T(8,128)(2,1)S(1)} %halves.1.refs_2_), channel_id=1, source_target_pairs={{0,2},{2,0},{4,6},{6,4},{8,16},{10,18},{12,20},{14,22},{16,8},{18,... | collective-permute-start | bytes 786440 | tf_op jit(solution)/shard_map/ppermute | solution.py:458
  11.4 15.5 %collective-permute-start.4 = (bf16[2,2,2,64,256]{4,3,2,1,0:T(8,128)(2,1)S(1)}, bf16[2,2,2,64,256]{4,3,2,1,0:T(8,128)(2,1)S(1)}, u32[]{:S(2)}, u32[]{:S(2)}) collective-permute-start(bf16[2,2,2,64,256]{4,3,2,1,0:T(8,128)(2,1)S(1)} %halves.1.refs_2_), channel_id=1, source_target_pairs={{0,4},{2,6},{4,0},{6,2},{8,12},{10,14},{12,8},{14,10},{16,20},{18,... | collective-permute-start | bytes 786440 | tf_op jit(solution)/shard_map/ppermute | solution.py:451
  14.0 13.2 %collective-permute-start.3 = (bf16[2,2,2,64,256]{4,3,2,1,0:T(8,128)(2,1)S(1)}, bf16[2,2,2,64,256]{4,3,2,1,0:T(8,128)(2,1)S(1)}, u32[]{:S(2)}, u32[]{:S(2)}) collective-permute-start(bf16[2,2,2,64,256]{4,3,2,1,0:T(8,128)(2,1)S(1)} %halves.1.refs_2_), channel_id=1, source_target_pairs={{0,8},{2,10},{4,12},{6,14},{8,0},{10,2},{12,4},{14,6},{16,24},{18,... | collective-permute-start | bytes 786440 | tf_op jit(solution)/shard_map/ppermute | solution.py:451
  21.9 5.0 %collective-permute-start.7 = (bf16[2,2,64,256]{3,2,1,0:T(8,128)(2,1)S(1)}, bf16[2,2,64,256]{3,2,1,0:T(8,128)(2,1)S(1)}, u32[]{:S(2)}, u32[]{:S(2)}) collective-permute-start(bf16[2,2,64,256]{3,2,1,0:T(8,128)(2,1)S(1)} %collective-permute-done.6.refs_4_), channel_id=1, source_target_pairs={{0,1},{1,0},{2,3},{3,2},{4,5},{5,4},{6,7},{7,6},{8,9},{9,8},{10,11... | collective-permute-start | bytes 393224 | tf_op jit(solution)/shard_map/ppermute | solution.py:491
  27.3 3.4 %collective-permute-start.8 = (bf16[5,2,2,2,64,256]{5,4,3,2,1,0:T(8,128)(2,1)S(1)}, bf16[5,2,2,2,64,256]{5,4,3,2,1,0:T(8,128)(2,1)S(1)}, u32[]{:S(2)}, u32[]{:S(2)}) collective-permute-start(bf16[5,2,2,2,64,256]{5,4,3,2,1,0:T(8,128)(2,1)S(1)} %groups.1.mine), channel_id=1, source_target_pairs={{0,2},{2,0},{4,6},{6,4},{8,10},{10,8},{12,14},{14,12},{16,18},{18,... | collective-permute-start | bytes 3932168 | tf_op jit(solution)/shard_map/ppermute | solution.py:451
  27.4 3.3 %copy-start.4 = (bf16[2,512,512]{2,1,0:T(8,128)(2,1)S(1)}, bf16[2,512,512]{2,1,0:T(8,128)(2,1)}, u32[]{:S(2)}) copy-start(bf16[2,512,512]{2,1,0:T(8,128)(2,1)} %constant.8.clone.near) | copy-start | bytes 3145732
  27.4 11.4 %collective-permute-start.9 = (bf16[256,512]{1,0:T(8,128)(2,1)S(1)}, bf16[256,512]{1,0:T(8,128)(2,1)S(1)}, u32[]{:S(2)}, u32[]{:S(2)}) collective-permute-start(bf16[256,512]{1,0:T(8,128)(2,1)S(1)} %get-tuple-element.47), channel_id=1, source_target_pairs={{0,9},{1,8},{2,11},{3,10},{4,13},{5,12},{6,15},{7,14},{8,17},{9,16... | collective-permute-start | bytes 786440 | tf_op jit(solution)/shard_map/ppermute | solution.py:471
  39.1 3.1 %collective-permute-start.10 = (bf16[5,2,2,2,64,256]{5,4,3,2,1,0:T(8,128)(2,1)S(1)}, bf16[5,2,2,2,64,256]{5,4,3,2,1,0:T(8,128)(2,1)S(1)}, u32[]{:S(2)}, u32[]{:S(2)}) collective-permute-start(bf16[5,2,2,2,64,256]{5,4,3,2,1,0:T(8,128)(2,1)S(1)} %get-tuple-element.52), channel_id=1, source_target_pairs={{0,2},{2,0},{4,6},{6,4},{8,10},{10,8},{12,14},{14,12},{16,18},{18,... | collective-permute-start | bytes 3932168 | tf_op jit(solution)/shard_map/ppermute | solution.py:451
  42.5 13.7 %collective-permute-start.11 = (bf16[2,2,2,64,256]{4,3,2,1,0:T(8,128)(2,1)S(1)}, bf16[2,2,2,64,256]{4,3,2,1,0:T(8,128)(2,1)S(1)}, u32[]{:S(2)}, u32[]{:S(2)}) collective-permute-start(bf16[2,2,2,64,256]{4,3,2,1,0:T(8,128)(2,1)S(1)} %get-tuple-element.53), channel_id=1, source_target_pairs={{0,4},{2,6},{4,0},{6,2},{8,12},{10,14},{12,8},{14,10},{16,20},{18,... | collective-permute-start | bytes 786440 | tf_op jit(solution)/shard_map/ppermute | solution.py:451
  46.2 10.3 %collective-permute-start.12 = (bf16[2,2,2,64,256]{4,3,2,1,0:T(8,128)(2,1)S(1)}, bf16[2,2,2,64,256]{4,3,2,1,0:T(8,128)(2,1)S(1)}, u32[]{:S(2)}, u32[]{:S(2)}) collective-permute-start(bf16[2,2,2,64,256]{4,3,2,1,0:T(8,128)(2,1)S(1)} %get-tuple-element.54), channel_id=1, source_target_pairs={{0,8},{2,10},{4,12},{6,14},{8,0},{10,2},{12,4},{14,6},{16,24},{18,... | collective-permute-start | bytes 786440 | tf_op jit(solution)/shard_map/ppermute | solution.py:451
  50.2 6.3 %collective-permute-start.13 = (bf16[2,2,2,64,256]{4,3,2,1,0:T(8,128)(2,1)S(1)}, bf16[2,2,2,64,256]{4,3,2,1,0:T(8,128)(2,1)S(1)}, u32[]{:S(2)}, u32[]{:S(2)}) collective-permute-start(bf16[2,2,2,64,256]{4,3,2,1,0:T(8,128)(2,1)S(1)} %get-tuple-element.55), channel_id=1, source_target_pairs={{0,2},{2,0},{4,6},{6,4},{8,16},{10,18},{12,20},{14,22},{16,8},{18,... | collective-permute-start | bytes 786440 | tf_op jit(solution)/shard_map/ppermute | solution.py:458
  50.2 5.9 %collective-permute-start.14 = (bf16[2,2,64,256]{3,2,1,0:T(8,128)(2,1)S(1)}, bf16[2,2,64,256]{3,2,1,0:T(8,128)(2,1)S(1)}, u32[]{:S(2)}, u32[]{:S(2)}) collective-permute-start(bf16[2,2,64,256]{3,2,1,0:T(8,128)(2,1)S(1)} %get-tuple-element.58), channel_id=1, source_target_pairs={{0,1},{1,0},{2,3},{3,2},{4,5},{5,4},{6,7},{7,6},{8,9},{9,8},{10,11... | collective-permute-start | bytes 393224 | tf_op jit(solution)/shard_map/ppermute | solution.py:519
  56.2 1.4 %collective-permute-start.16 = (bf16[2,2,64,256]{3,2,1,0:T(8,128)(2,1)S(1)}, bf16[2,2,64,256]{3,2,1,0:T(8,128)(2,1)S(1)}, u32[]{:S(2)}, u32[]{:S(2)}) collective-permute-start(bf16[2,2,64,256]{3,2,1,0:T(8,128)(2,1)S(1)} %near.3), channel_id=1, source_target_pairs={{0,2},{2,0},{4,8},{6,10},{8,4},{10,6},{12,16},{14,18},{16,12},{18,... | collective-permute-start | bytes 393224 | tf_op jit(solution)/shard_map/ppermute | solution.py:458
  56.7 5.7 %collective-permute-start.15 = (bf16[2,2,64,256]{3,2,1,0:T(8,128)(2,1)S(1)}, bf16[2,2,64,256]{3,2,1,0:T(8,128)(2,1)S(1)}, u32[]{:S(2)}, u32[]{:S(2)}) collective-permute-start(bf16[2,2,64,256]{3,2,1,0:T(8,128)(2,1)S(1)} %get-tuple-element.61), channel_id=1, source_target_pairs={{0,1},{1,0},{2,3},{3,2},{4,5},{5,4},{6,7},{7,6},{8,9},{9,8},{10,11... | collective-permute-start | bytes 393224 | tf_op jit(solution)/shard_map/ppermute | solution.py:530

commit v2 on v0

--- a/solution.py
+++ b/solution.py
@@ -291,13 +291,24 @@
         odd = left(parts_of(far_far, everything, high), True, rows_buf[size : 2 * size, :])
         er, ei = both(plus(even, odd), less(even, odd), 0)
         br, bi = patch(1, 0), patch(1, 1)
-        put_cols(cols_buf, (br * er + bi * ei, br * ei - bi * er))
+        grad = (br * er + bi * ei, br * ei - bi * er)
         wr, wi = pair_of(psi2)
         put_term(1, 0, wr * er + wi * ei)
         put_term(1, 1, wr * ei - wi * er)
-        near_parts = parts_of(near, everything, everything)
-        put_rows(rows_buf, right(near_parts, True, cols_buf[...]))
-        gr, gi = left(near_parts, True, rows_buf[...])
+        firsts = [near[c, low, low].astype(f32) * 0.5 for c in range(2)]
+        seconds = [near[c, low, high].astype(f32) * 0.5 for c in range(2)]
+        evens = [x.astype(bf16) for x in plus(firsts, seconds)]
+        odds = [x.astype(bf16) for x in less(firsts, seconds)]
+        one, two = [x[:, low] for x in grad], [x[:, high] for x in grad]
+        put_col_halves(cols_buf, plus(one, two), less(one, two))
+        even = right(evens, True, cols_buf[:, 0:size])
+        odd = right(odds, True, cols_buf[:, size : 2 * size])
+        back2 = both(plus(even, odd), less(even, odd), 1)
+        one, two = [x[low] for x in back2], [x[high] for x in back2]
+        put_row_halves(rows_buf, plus(one, two), less(one, two))
+        even = left(evens, True, rows_buf[0:size, :])
+        odd = left(odds, True, rows_buf[size : 2 * size, :])
+        gr, gi = both(plus(even, odd), less(even, odd), 0)
         pr, pi = pair_of(probe)
         put_term(0, 0, pr * gr + pi * gi)
         put_term(0, 1, pr * gi - pi * gr)

time: 62.4 us -> 61.7 us (0.989)
  waiting for transfers between devices: 39 us -> 38 us
    ppermute x6, starting transfers between devices: 9.73 us -> 9.06 us  [paired_with(): lax.ppermute(value, 'tile', [(one, one ^ unit) for one in range(count)])]
where the time goes in v2:
time: 61.7 us; the launch traced here: 61.5 us
  waiting for transfers between devices  38 us (62%)
  starting transfers between devices  16 us (26%)
  Pallas kernels  3.04 us (5%)
  local copies, waits for them, and re-layouts  1.9 us (3%)
  other arithmetic  1.7 us (3%)
  between operations  0.82 us (1%)
    ppermute x6, waiting for transfers between devices, paired_with(): lax.ppermute(value, 'tile', [(one, one ^ unit) for one in range(count)])  11.2 us
    ppermute x6, starting transfers between devices, paired_with(): lax.ppermute(value, 'tile', [(one, one ^ unit) for one in range(count)])  9.06 us
    ppermute x1, waiting for transfers between devices, shards(): lax.ppermute(crossed, ('tile', 'scan'), [(2 * a + x, 2 * b + 1 - x) for a...  8.26 us
    ppermute x1, waiting for transfers between devices, shards(): half_got = lax.ppermute(half_away, 'scan', swap)  5.37 us
    ppermute x1, waiting for transfers between devices, shards(): lax.ppermute(away, 'scan', swap)  4.78 us
    ppermute x1, waiting for transfers between devices, brought(): return lax.ppermute(value, 'tile', ahead_pairs)  4.56 us
    ppermute x1, waiting for transfers between devices, shards(): probe_pieces = [probe_wave, lax.ppermute(probe_wave, 'scan', swap)]  3.47 us
    ppermute x1, starting transfers between devices, shards(): beside = lax.ppermute(own, 'scan', swap)  3 us
  transfers between devices with their start and end apart: 16, of which 11 were waited for; matrix products, arithmetic and copies ran while one was open for 0% of the time, Pallas kernels for 4%

profile of v2, /device:TPU:0, one launch (start us, length us, event | category | flops | bytes accessed | tf_op | source)
XLA Modules:
  0.0 61.5 jit_solution(18421494514770435239)
XLA Ops:
  0.0 1.0 %convert_element_type.9.refs_0_ = bf16[2,2,64,256]{3,2,1,0:T(8,128)(2,1)S(1)} convert(f32[2,2,64,256]{3,2,1,0:T(8,128)} %param.8) | non-fusion elementwise | flops 65536 | bytes 393216 | tf_op jit(solution)/shard_map/convert_element_type | solution.py:459
  1.0 3.0 %collective-permute-start = (bf16[2,2,64,256]{3,2,1,0:T(8,128)(2,1)S(1)}, bf16[2,2,64,256]{3,2,1,0:T(8,128)(2,1)S(1)}, u32[]{:S(2)}, u32[]{:S(2)}) collective-permute-start(bf16[2,2,64,256]{3,2,1,0:T(8,128)(2,1)S(1)} %convert_element_type.9.refs_0_), channel_id=1, source_target_pairs={{0,1},{1,0},{2,3},{3,2},{4,5},{5,4},{6,7},{7,6},{8,9},{9,8},{10,11... | collective-permute-start | bytes 393224 | tf_op jit(solution)/shard_map/ppermute | solution.py:462
  4.6 1.2 %copy-done = f32[2,256,512]{2,1,0:T(8,128)S(1)} copy-done((f32[2,256,512]{2,1,0:T(8,128)S(1)}, f32[2,256,512]{2,1,0:T(8,128)}, u32[]{:S(2)}) %copy-start) | copy-done | bytes 1048600
  5.9 0.7 %copy-done.1 = s32[2]{0:T(128)S(1)} copy-done((s32[2]{0:T(128)S(1)}, s32[2]{0:T(128)}, u32[]{:S(2)}) %copy-start.1) | copy-done | bytes 32
  6.5 0.6 messages.1
  7.1 1.6 %collective-permute-start.2 = (bf16[272,512]{1,0:T(8,128)(2,1)S(1)}, bf16[272,512]{1,0:T(8,128)(2,1)S(1)}, u32[]{:S(2)}, u32[]{:S(2)}) collective-permute-start(bf16[272,512]{1,0:T(8,128)(2,1)S(1)} %get-tuple-element.34), channel_id=1, source_target_pairs={{0,8},{2,10},{4,12},{6,14},{8,16},{10,18},{12,20},{14,22},{16,24},... | collective-permute-start | bytes 835592 | tf_op jit(solution)/shard_map/ppermute | solution.py:447
  8.7 0.5 collective-permute-start.1
  9.3 0.1 collective-permute-start.6
  9.4 0.5 collective-permute-start.5
  9.9 4.1 %collective-permute-start.4 = (bf16[2,2,2,64,256]{4,3,2,1,0:T(8,128)(2,1)S(1)}, bf16[2,2,2,64,256]{4,3,2,1,0:T(8,128)(2,1)S(1)}, u32[]{:S(2)}, u32[]{:S(2)}) collective-permute-start(bf16[2,2,2,64,256]{4,3,2,1,0:T(8,128)(2,1)S(1)} %halves.1.refs_2_), channel_id=1, source_target_pairs={{0,4},{2,6},{4,0},{6,2},{8,12},{10,14},{12,8},{14,10},{16,20},{18,... | collective-permute-start | bytes 786440 | tf_op jit(solution)/shard_map/ppermute | solution.py:450
  14.0 4.6 %collective-permute-done.2.notes.refs_0_ = bf16[272,512]{1,0:T(8,128)(2,1)S(1)} collective-permute-done((bf16[272,512]{1,0:T(8,128)(2,1)S(1)}, bf16[272,512]{1,0:T(8,128)(2,1)S(1)}, u32[]{:S(2)}, u32[]{:S(2)}) %collective-permute-start.2) | collective-permute-done | bytes 278560 | tf_op jit(solution)/shard_map/ppermute | solution.py:447
  18.6 3.5 %collective-permute-done.1.refs_1_ = bf16[2,512,256]{2,1,0:T(8,128)(2,1)S(1)} collective-permute-done((bf16[2,512,256]{2,1,0:T(8,128)(2,1)}, bf16[2,512,256]{2,1,0:T(8,128)(2,1)S(1)}, u32[]{:S(2)}, u32[]{:S(2)}) %collective-permute-start.1) | collective-permute-done | bytes 524320 | tf_op jit(solution)/shard_map/ppermute | solution.py:465
  22.1 1.7 %collective-permute-done.4.refs_1_ = bf16[2,2,2,64,256]{4,3,2,1,0:T(8,128)(2,1)S(1)} collective-permute-done((bf16[2,2,2,64,256]{4,3,2,1,0:T(8,128)(2,1)S(1)}, bf16[2,2,2,64,256]{4,3,2,1,0:T(8,128)(2,1)S(1)}, u32[]{:S(2)}, u32[]{:S(2)}) %collective-permute-start.4) | collective-permute-done | bytes 262176 | tf_op jit(solution)/shard_map/ppermute | solution.py:450
  23.8 4.7 %collective-permute-done.3.refs_0_ = bf16[2,2,2,64,256]{4,3,2,1,0:T(8,128)(2,1)S(1)} collective-permute-done((bf16[2,2,2,64,256]{4,3,2,1,0:T(8,128)(2,1)S(1)}, bf16[2,2,2,64,256]{4,3,2,1,0:T(8,128)(2,1)S(1)}, u32[]{:S(2)}, u32[]{:S(2)}) %collective-permute-start.3) | collective-permute-done | bytes 262176 | tf_op jit(solution)/shard_map/ppermute | solution.py:450
  28.5 0.1 groups.1.mine
  28.6 0.1 collective-permute-start.7
  28.8 1.4 %rolled.1 = (bf16[2,512,512]{2,1,0:T(8,128)(2,1)S(1)}, bf16[2,512,256]{2,1,0:T(8,128)(2,1)S(1)}, bf16[2,256,512]{2,1,0:T(8,128)(2,1)S(1)}) custom-call(bf16[272,512]{1,0:T(8,128)(2,1)S(1)} %collective-permute-done.2.notes.refs_0_, bf16[2,512,512]{2,1,0:T(8,128)(2,1)S(1)} %copy-done.3, bf16[2,512,512]{2,1,0:T(8,128)(2,1)S(1)} %copy-done.5, ...), custom_call_target="tpu_custom_call" | custom-call | flops 8589934592 | bytes 6291456 | tf_op jit(solution)/shard_map/rolled/pallas_call | solution.py:133
  30.3 1.5 %collective-permute-done.7.theirs = bf16[5,2,2,2,64,256]{5,4,3,2,1,0:T(8,128)(2,1)S(1)} collective-permute-done((bf16[5,2,2,2,64,256]{5,4,3,2,1,0:T(8,128)(2,1)S(1)}, bf16[5,2,2,2,64,256]{5,4,3,2,1,0:T(8,128)(2,1)S(1)}, u32[]{:S(2)}, u32[]{:S(2)}) %collective-permute-start.7) | collective-permute-done | bytes 1310752 | tf_op jit(solution)/shard_map/ppermute | solution.py:450
  31.7 0.1 forth.1
  31.9 8.3 %collective-permute-done.8.refs_1_ = bf16[256,512]{1,0:T(8,128)(2,1)S(1)} collective-permute-done((bf16[256,512]{1,0:T(8,128)(2,1)S(1)}, bf16[256,512]{1,0:T(8,128)(2,1)S(1)}, u32[]{:S(2)}, u32[]{:S(2)}) %collective-permute-start.8) | collective-permute-done | bytes 262176 | tf_op jit(solution)/shard_map/ppermute | solution.py:468
  40.1 0.3 back.1
  40.5 3.0 %collective-permute-done.9.got = bf16[5,2,2,2,64,256]{5,4,3,2,1,0:T(8,128)(2,1)S(1)} collective-permute-done((bf16[5,2,2,2,64,256]{5,4,3,2,1,0:T(8,128)(2,1)S(1)}, bf16[5,2,2,2,64,256]{5,4,3,2,1,0:T(8,128)(2,1)S(1)}, u32[]{:S(2)}, u32[]{:S(2)}) %collective-permute-start.9) | collective-permute-done | bytes 1310752 | tf_op jit(solution)/shard_map/ppermute | solution.py:450
  43.5 0.3 merge.1
  43.9 4.7 %collective-permute-start.11 = (bf16[2,2,2,64,256]{4,3,2,1,0:T(8,128)(2,1)S(1)}, bf16[2,2,2,64,256]{4,3,2,1,0:T(8,128)(2,1)S(1)}, u32[]{:S(2)}, u32[]{:S(2)}) collective-permute-start(bf16[2,2,2,64,256]{4,3,2,1,0:T(8,128)(2,1)S(1)} %get-tuple-element.50), channel_id=1, source_target_pairs={{0,8},{2,10},{4,12},{6,14},{8,0},{10,2},{12,4},{14,6},{16,24},{18,... | collective-permute-start | bytes 786440 | tf_op jit(solution)/shard_map/ppermute | solution.py:450
  48.6 0.5 collective-permute-start.13
  49.1 5.4 %collective-permute-done.13.got = bf16[2,2,64,256]{3,2,1,0:T(8,128)(2,1)S(1)} collective-permute-done((bf16[2,2,64,256]{3,2,1,0:T(8,128)(2,1)S(1)}, bf16[2,2,64,256]{3,2,1,0:T(8,128)(2,1)S(1)}, u32[]{:S(2)}, u32[]{:S(2)}) %collective-permute-start.13) | collective-permute-done | bytes 131104 | tf_op jit(solution)/shard_map/ppermute | solution.py:509
  54.6 0.3 collective-permute-done.11.refs_1_
  54.9 0.1 sums.1
  55.1 0.6 collective-permute-start.14
  55.7 0.3 collective-permute-done.15
  56.0 4.8 %collective-permute-done.14 = bf16[2,2,64,256]{3,2,1,0:T(8,128)(2,1)S(1)} collective-permute-done((bf16[2,2,64,256]{3,2,1,0:T(8,128)(2,1)S(1)}, bf16[2,2,64,256]{3,2,1,0:T(8,128)(2,1)S(1)}, u32[]{:S(2)}, u32[]{:S(2)}) %collective-permute-start.14) | collective-permute-done | bytes 131104 | tf_op jit(solution)/shard_map/ppermute | solution.py:520
  60.8 0.7 %convert_add_fusion = f32[2,2,64,256]{3,2,1,0:T(8,128)} fusion(bf16[2,2,64,256]{3,2,1,0:T(8,128)(2,1)S(1)} %collective-permute-done.15, f32[2,2,64,256]{3,2,1,0:T(8,128)S(1)} %get-tuple-element.56, bf16[2,2,64,256]{3,2,1,0:T(8,128)(2,1)S(1)} %collective-permute-done.14), kind=kLoop, calls=%fused_computation | loop fusion | flops 262144 | bytes 786432 | tf_op jit(solution)/shard_map/add | solution.py:521
  (23 shorter events, 0.3 us)
Async XLA Ops:
  1.0 7.8 %collective-permute-start = (bf16[2,2,64,256]{3,2,1,0:T(8,128)(2,1)S(1)}, bf16[2,2,64,256]{3,2,1,0:T(8,128)(2,1)S(1)}, u32[]{:S(2)}, u32[]{:S(2)}) collective-permute-start(bf16[2,2,64,256]{3,2,1,0:T(8,128)(2,1)S(1)} %convert_element_type.9.refs_0_), channel_id=1, source_target_pairs={{0,1},{1,0},{2,3},{3,2},{4,5},{5,4},{6,7},{7,6},{8,9},{9,8},{10,11... | collective-permute-start | bytes 393224 | tf_op jit(solution)/shard_map/ppermute | solution.py:462
  4.6 1.2 %copy-start = (f32[2,256,512]{2,1,0:T(8,128)S(1)}, f32[2,256,512]{2,1,0:T(8,128)}, u32[]{:S(2)}) copy-start(f32[2,256,512]{2,1,0:T(8,128)} %amps.1) | copy-start | bytes 3145732
  5.9 0.7 %copy-start.1 = (s32[2]{0:T(128)S(1)}, s32[2]{0:T(128)}, u32[]{:S(2)}) copy-start(s32[2]{0:T(128)} %offsets.1) | copy-start | bytes 28
  7.1 11.5 %collective-permute-start.2 = (bf16[272,512]{1,0:T(8,128)(2,1)S(1)}, bf16[272,512]{1,0:T(8,128)(2,1)S(1)}, u32[]{:S(2)}, u32[]{:S(2)}) collective-permute-start(bf16[272,512]{1,0:T(8,128)(2,1)S(1)} %get-tuple-element.34), channel_id=1, source_target_pairs={{0,8},{2,10},{4,12},{6,14},{8,16},{10,18},{12,20},{14,22},{16,24},... | collective-permute-start | bytes 835592 | tf_op jit(solution)/shard_map/ppermute | solution.py:447
  8.7 13.3 %collective-permute-start.1 = (bf16[2,512,256]{2,1,0:T(8,128)(2,1)}, bf16[2,512,256]{2,1,0:T(8,128)(2,1)S(1)}, u32[]{:S(2)}, u32[]{:S(2)}) collective-permute-start(bf16[2,512,256]{2,1,0:T(8,128)(2,1)} %refs_0_), channel_id=1, source_target_pairs={{0,1},{1,0},{2,3},{3,2},{4,5},{5,4},{6,7},{7,6},{8,9},{9,8},{10,11... | collective-permute-start | bytes 1572872 | tf_op jit(solution)/shard_map/ppermute | solution.py:465
  9.3 19.5 %copy-start.2 = (bf16[2,512,256]{2,1,0:T(8,128)(2,1)S(1)}, bf16[2,512,256]{2,1,0:T(8,128)(2,1)}, u32[]{:S(2)}) copy-start(bf16[2,512,256]{2,1,0:T(8,128)(2,1)} %refs_0_) | copy-start | bytes 1572868
  9.3 19.5 %copy-start.3 = (bf16[2,512,512]{2,1,0:T(8,128)(2,1)S(1)}, bf16[2,512,512]{2,1,0:T(8,128)(2,1)}, u32[]{:S(2)}) copy-start(bf16[2,512,512]{2,1,0:T(8,128)(2,1)} %constant.6.clone.far_rows) | copy-start | bytes 3145732
  9.3 19.5 %copy-start.5 = (bf16[2,512,512]{2,1,0:T(8,128)(2,1)S(1)}, bf16[2,512,512]{2,1,0:T(8,128)(2,1)}, u32[]{:S(2)}) copy-start(bf16[2,512,512]{2,1,0:T(8,128)(2,1)} %constant.7.clone.far_cols) | copy-start | bytes 3145732
  9.3 12.7 %collective-permute-start.6 = (bf16[2,2,2,64,256]{4,3,2,1,0:T(8,128)(2,1)S(1)}, bf16[2,2,2,64,256]{4,3,2,1,0:T(8,128)(2,1)S(1)}, u32[]{:S(2)}, u32[]{:S(2)}) collective-permute-start(bf16[2,2,2,64,256]{4,3,2,1,0:T(8,128)(2,1)S(1)} %halves.1.refs_2_), channel_id=1, source_target_pairs={{0,2},{2,0},{4,6},{6,4},{8,16},{10,18},{12,20},{14,22},{16,8},{18,... | collective-permute-start | bytes 786440 | tf_op jit(solution)/shard_map/ppermute | solution.py:457
  9.4 12.6 %collective-permute-start.5 = (bf16[2,2,2,64,256]{4,3,2,1,0:T(8,128)(2,1)S(1)}, bf16[2,2,2,64,256]{4,3,2,1,0:T(8,128)(2,1)S(1)}, u32[]{:S(2)}, u32[]{:S(2)}) collective-permute-start(bf16[2,2,2,64,256]{4,3,2,1,0:T(8,128)(2,1)S(1)} %halves.1.refs_2_), channel_id=1, source_target_pairs={{0,2},{2,0},{4,8},{6,10},{8,4},{10,6},{12,16},{14,18},{16,12},{18,... | collective-permute-start | bytes 786440 | tf_op jit(solution)/shard_map/ppermute | solution.py:457
  9.9 13.9 %collective-permute-start.4 = (bf16[2,2,2,64,256]{4,3,2,1,0:T(8,128)(2,1)S(1)}, bf16[2,2,2,64,256]{4,3,2,1,0:T(8,128)(2,1)S(1)}, u32[]{:S(2)}, u32[]{:S(2)}) collective-permute-start(bf16[2,2,2,64,256]{4,3,2,1,0:T(8,128)(2,1)S(1)} %halves.1.refs_2_), channel_id=1, source_target_pairs={{0,4},{2,6},{4,0},{6,2},{8,12},{10,14},{12,8},{14,10},{16,20},{18,... | collective-permute-start | bytes 786440 | tf_op jit(solution)/shard_map/ppermute | solution.py:450
  18.6 9.9 %collective-permute-start.3 = (bf16[2,2,2,64,256]{4,3,2,1,0:T(8,128)(2,1)S(1)}, bf16[2,2,2,64,256]{4,3,2,1,0:T(8,128)(2,1)S(1)}, u32[]{:S(2)}, u32[]{:S(2)}) collective-permute-start(bf16[2,2,2,64,256]{4,3,2,1,0:T(8,128)(2,1)S(1)} %halves.1.refs_2_), channel_id=1, source_target_pairs={{0,8},{2,10},{4,12},{6,14},{8,0},{10,2},{12,4},{14,6},{16,24},{18,... | collective-permute-start | bytes 786440 | tf_op jit(solution)/shard_map/ppermute | solution.py:450
  28.6 3.1 %collective-permute-start.7 = (bf16[5,2,2,2,64,256]{5,4,3,2,1,0:T(8,128)(2,1)S(1)}, bf16[5,2,2,2,64,256]{5,4,3,2,1,0:T(8,128)(2,1)S(1)}, u32[]{:S(2)}, u32[]{:S(2)}) collective-permute-start(bf16[5,2,2,2,64,256]{5,4,3,2,1,0:T(8,128)(2,1)S(1)} %groups.1.mine), channel_id=1, source_target_pairs={{0,2},{2,0},{4,6},{6,4},{8,10},{10,8},{12,14},{14,12},{16,18},{18,... | collective-permute-start | bytes 3932168 | tf_op jit(solution)/shard_map/ppermute | solution.py:450
  28.8 3.0 %copy-start.4 = (bf16[2,512,512]{2,1,0:T(8,128)(2,1)S(1)}, bf16[2,512,512]{2,1,0:T(8,128)(2,1)}, u32[]{:S(2)}) copy-start(bf16[2,512,512]{2,1,0:T(8,128)(2,1)} %constant.8.clone.near) | copy-start | bytes 3145732
  28.8 11.4 %collective-permute-start.8 = (bf16[256,512]{1,0:T(8,128)(2,1)S(1)}, bf16[256,512]{1,0:T(8,128)(2,1)S(1)}, u32[]{:S(2)}, u32[]{:S(2)}) collective-permute-start(bf16[256,512]{1,0:T(8,128)(2,1)S(1)} %get-tuple-element.43), channel_id=1, source_target_pairs={{0,9},{1,8},{2,11},{3,10},{4,13},{5,12},{6,15},{7,14},{8,17},{9,16... | collective-permute-start | bytes 786440 | tf_op jit(solution)/shard_map/ppermute | solution.py:468
  40.4 3.1 %collective-permute-start.9 = (bf16[5,2,2,2,64,256]{5,4,3,2,1,0:T(8,128)(2,1)S(1)}, bf16[5,2,2,2,64,256]{5,4,3,2,1,0:T(8,128)(2,1)S(1)}, u32[]{:S(2)}, u32[]{:S(2)}) collective-permute-start(bf16[5,2,2,2,64,256]{5,4,3,2,1,0:T(8,128)(2,1)S(1)} %get-tuple-element.48), channel_id=1, source_target_pairs={{0,2},{2,0},{4,6},{6,4},{8,10},{10,8},{12,14},{14,12},{16,18},{18,... | collective-permute-start | bytes 3932168 | tf_op jit(solution)/shard_map/ppermute | solution.py:450
  43.8 10.8 %collective-permute-start.10 = (bf16[2,2,2,64,256]{4,3,2,1,0:T(8,128)(2,1)S(1)}, bf16[2,2,2,64,256]{4,3,2,1,0:T(8,128)(2,1)S(1)}, u32[]{:S(2)}, u32[]{:S(2)}) collective-permute-start(bf16[2,2,2,64,256]{4,3,2,1,0:T(8,128)(2,1)S(1)} %get-tuple-element.49), channel_id=1, source_target_pairs={{0,4},{2,6},{4,0},{6,2},{8,12},{10,14},{12,8},{14,10},{16,20},{18,... | collective-permute-start | bytes 786440 | tf_op jit(solution)/shard_map/ppermute | solution.py:450
  43.9 11.0 %collective-permute-start.11 = (bf16[2,2,2,64,256]{4,3,2,1,0:T(8,128)(2,1)S(1)}, bf16[2,2,2,64,256]{4,3,2,1,0:T(8,128)(2,1)S(1)}, u32[]{:S(2)}, u32[]{:S(2)}) collective-permute-start(bf16[2,2,2,64,256]{4,3,2,1,0:T(8,128)(2,1)S(1)} %get-tuple-element.50), channel_id=1, source_target_pairs={{0,8},{2,10},{4,12},{6,14},{8,0},{10,2},{12,4},{14,6},{16,24},{18,... | collective-permute-start | bytes 786440 | tf_op jit(solution)/shard_map/ppermute | solution.py:450
  48.6 6.3 %collective-permute-start.12 = (bf16[2,2,2,64,256]{4,3,2,1,0:T(8,128)(2,1)S(1)}, bf16[2,2,2,64,256]{4,3,2,1,0:T(8,128)(2,1)S(1)}, u32[]{:S(2)}, u32[]{:S(2)}) collective-permute-start(bf16[2,2,2,64,256]{4,3,2,1,0:T(8,128)(2,1)S(1)} %get-tuple-element.51), channel_id=1, source_target_pairs={{0,2},{2,0},{4,6},{6,4},{8,16},{10,18},{12,20},{14,22},{16,8},{18,... | collective-permute-start | bytes 786440 | tf_op jit(solution)/shard_map/ppermute | solution.py:457
  48.6 5.9 %collective-permute-start.13 = (bf16[2,2,64,256]{3,2,1,0:T(8,128)(2,1)S(1)}, bf16[2,2,64,256]{3,2,1,0:T(8,128)(2,1)S(1)}, u32[]{:S(2)}, u32[]{:S(2)}) collective-permute-start(bf16[2,2,64,256]{3,2,1,0:T(8,128)(2,1)S(1)} %get-tuple-element.54), channel_id=1, source_target_pairs={{0,1},{1,0},{2,3},{3,2},{4,5},{5,4},{6,7},{7,6},{8,9},{9,8},{10,11... | collective-permute-start | bytes 393224 | tf_op jit(solution)/shard_map/ppermute | solution.py:509
  54.6 1.4 %collective-permute-start.15 = (bf16[2,2,64,256]{3,2,1,0:T(8,128)(2,1)S(1)}, bf16[2,2,64,256]{3,2,1,0:T(8,128)(2,1)S(1)}, u32[]{:S(2)}, u32[]{:S(2)}) collective-permute-start(bf16[2,2,64,256]{3,2,1,0:T(8,128)(2,1)S(1)} %near.3), channel_id=1, source_target_pairs={{0,2},{2,0},{4,8},{6,10},{8,4},{10,6},{12,16},{14,18},{16,12},{18,... | collective-permute-start | bytes 393224 | tf_op jit(solution)/shard_map/ppermute | solution.py:457
  55.1 5.7 %collective-permute-start.14 = (bf16[2,2,64,256]{3,2,1,0:T(8,128)(2,1)S(1)}, bf16[2,2,64,256]{3,2,1,0:T(8,128)(2,1)S(1)}, u32[]{:S(2)}, u32[]{:S(2)}) collective-permute-start(bf16[2,2,64,256]{3,2,1,0:T(8,128)(2,1)S(1)} %get-tuple-element.57), channel_id=1, source_target_pairs={{0,1},{1,0},{2,3},{3,2},{4,5},{5,4},{6,7},{7,6},{8,9},{9,8},{10,11... | collective-permute-start | bytes 393224 | tf_op jit(solution)/shard_map/ppermute | solution.py:520

commit v3 on v2

--- a/solution.py
+++ b/solution.py
@@ -225,12 +225,23 @@
     @pl.when(live)
     def _():
         _, _, patch = tile_access(span, tile_rows, offset, core, mine, theirs)
-        near_parts = parts_of(near, everything, everything)
+        firsts = [near[c, low, low].astype(f32) * 0.5 for c in range(2)]
+        seconds = [near[c, low, high].astype(f32) * 0.5 for c in range(2)]
+        evens = [x.astype(bf16) for x in plus(firsts, seconds)]
+        odds = [x.astype(bf16) for x in less(firsts, seconds)]
         pr, pi = pair_of(probe)
         ar, ai = patch(0, 0), patch(0, 1)
-        put_rows(rows_buf, (pr * ar - pi * ai, pr * ai + pi * ar))
-        put_cols(cols_buf, left(near_parts, False, rows_buf[...]))
-        two = right(near_parts, False, cols_buf[...])
+        psi1 = (pr * ar - pi * ai, pr * ai + pi * ar)
+        top, bottom = [x[low] for x in psi1], [x[high] for x in psi1]
+        put_row_halves(rows_buf, plus(top, bottom), less(top, bottom))
+        even = left(evens, False, rows_buf[0:size, :])
+        odd = left(odds, False, rows_buf[size : 2 * size, :])
+        half1 = both(plus(even, odd), less(even, odd), 0)
+        top, bottom = [x[:, low] for x in half1], [x[:, high] for x in half1]
+        put_col_halves(cols_buf, plus(top, bottom), less(top, bottom))
+        even = right(evens, False, cols_buf[:, 0:size])
+        odd = right(odds, False, cols_buf[:, size : 2 * size])
+        two = both(plus(even, odd), less(even, odd), 1)
         psi2[0] = two[0].astype(bf16)
         psi2[1] = two[1].astype(bf16)
         wr, wi = pair_of(psi2)

time: 61.7 us -> 61.7 us (level)
  no operation moved by 1% of the time
where the time goes in v3:
time: 61.7 us; the launch traced here: 61.5 us
  waiting for transfers between devices  38 us (62%)
  starting transfers between devices  16 us (26%)
  Pallas kernels  3.04 us (5%)
  local copies, waits for them, and re-layouts  1.9 us (3%)
  other arithmetic  1.7 us (3%)
  between operations  0.82 us (1%)
    ppermute x6, waiting for transfers between devices, paired_with(): lax.ppermute(value, 'tile', [(one, one ^ unit) for one in range(count)])  11.2 us
    ppermute x6, starting transfers between devices, paired_with(): lax.ppermute(value, 'tile', [(one, one ^ unit) for one in range(count)])  9.06 us
    ppermute x1, waiting for transfers between devices, shards(): lax.ppermute(crossed, ('tile', 'scan'), [(2 * a + x, 2 * b + 1 - x) for a...  8.26 us
    ppermute x1, waiting for transfers between devices, shards(): half_got = lax.ppermute(half_away, 'scan', swap)  5.37 us
    ppermute x1, waiting for transfers between devices, shards(): lax.ppermute(away, 'scan', swap)  4.78 us
    ppermute x1, waiting for transfers between devices, brought(): return lax.ppermute(value, 'tile', ahead_pairs)  4.56 us
    ppermute x1, waiting for transfers between devices, shards(): probe_pieces = [probe_wave, lax.ppermute(probe_wave, 'scan', swap)]  3.47 us
    ppermute x1, starting transfers between devices, shards(): beside = lax.ppermute(own, 'scan', swap)  3 us
  transfers between devices with their start and end apart: 16, of which 11 were waited for; matrix products, arithmetic and copies ran while one was open for 0% of the time, Pallas kernels for 4%

profile of v3, /device:TPU:0, one launch (start us, length us, event | category | flops | bytes accessed | tf_op | source)
XLA Modules:
  0.0 61.5 jit_solution(3558962989522076274)
XLA Ops:
  0.0 1.0 %convert_element_type.9.refs_0_ = bf16[2,2,64,256]{3,2,1,0:T(8,128)(2,1)S(1)} convert(f32[2,2,64,256]{3,2,1,0:T(8,128)} %param.8) | non-fusion elementwise | flops 65536 | bytes 393216 | tf_op jit(solution)/shard_map/convert_element_type | solution.py:470
  1.0 3.0 %collective-permute-start = (bf16[2,2,64,256]{3,2,1,0:T(8,128)(2,1)S(1)}, bf16[2,2,64,256]{3,2,1,0:T(8,128)(2,1)S(1)}, u32[]{:S(2)}, u32[]{:S(2)}) collective-permute-start(bf16[2,2,64,256]{3,2,1,0:T(8,128)(2,1)S(1)} %convert_element_type.9.refs_0_), channel_id=1, source_target_pairs={{0,1},{1,0},{2,3},{3,2},{4,5},{5,4},{6,7},{7,6},{8,9},{9,8},{10,11... | collective-permute-start | bytes 393224 | tf_op jit(solution)/shard_map/ppermute | solution.py:473
  4.6 1.2 %copy-done = f32[2,256,512]{2,1,0:T(8,128)S(1)} copy-done((f32[2,256,512]{2,1,0:T(8,128)S(1)}, f32[2,256,512]{2,1,0:T(8,128)}, u32[]{:S(2)}) %copy-start) | copy-done | bytes 1048600
  5.9 0.7 %copy-done.1 = s32[2]{0:T(128)S(1)} copy-done((s32[2]{0:T(128)S(1)}, s32[2]{0:T(128)}, u32[]{:S(2)}) %copy-start.1) | copy-done | bytes 32
  6.5 0.6 messages.1
  7.1 1.6 %collective-permute-start.2 = (bf16[272,512]{1,0:T(8,128)(2,1)S(1)}, bf16[272,512]{1,0:T(8,128)(2,1)S(1)}, u32[]{:S(2)}, u32[]{:S(2)}) collective-permute-start(bf16[272,512]{1,0:T(8,128)(2,1)S(1)} %get-tuple-element.34), channel_id=1, source_target_pairs={{0,8},{2,10},{4,12},{6,14},{8,16},{10,18},{12,20},{14,22},{16,24},... | collective-permute-start | bytes 835592 | tf_op jit(solution)/shard_map/ppermute | solution.py:458
  8.7 0.5 collective-permute-start.1
  9.3 0.1 collective-permute-start.6
  9.4 0.5 collective-permute-start.5
  9.9 4.1 %collective-permute-start.4 = (bf16[2,2,2,64,256]{4,3,2,1,0:T(8,128)(2,1)S(1)}, bf16[2,2,2,64,256]{4,3,2,1,0:T(8,128)(2,1)S(1)}, u32[]{:S(2)}, u32[]{:S(2)}) collective-permute-start(bf16[2,2,2,64,256]{4,3,2,1,0:T(8,128)(2,1)S(1)} %halves.1.refs_2_), channel_id=1, source_target_pairs={{0,4},{2,6},{4,0},{6,2},{8,12},{10,14},{12,8},{14,10},{16,20},{18,... | collective-permute-start | bytes 786440 | tf_op jit(solution)/shard_map/ppermute | solution.py:461
  14.0 4.6 %collective-permute-done.2.notes.refs_0_ = bf16[272,512]{1,0:T(8,128)(2,1)S(1)} collective-permute-done((bf16[272,512]{1,0:T(8,128)(2,1)S(1)}, bf16[272,512]{1,0:T(8,128)(2,1)S(1)}, u32[]{:S(2)}, u32[]{:S(2)}) %collective-permute-start.2) | collective-permute-done | bytes 278560 | tf_op jit(solution)/shard_map/ppermute | solution.py:458
  18.6 3.5 %collective-permute-done.1.refs_1_ = bf16[2,512,256]{2,1,0:T(8,128)(2,1)S(1)} collective-permute-done((bf16[2,512,256]{2,1,0:T(8,128)(2,1)}, bf16[2,512,256]{2,1,0:T(8,128)(2,1)S(1)}, u32[]{:S(2)}, u32[]{:S(2)}) %collective-permute-start.1) | collective-permute-done | bytes 524320 | tf_op jit(solution)/shard_map/ppermute | solution.py:476
  22.1 1.7 %collective-permute-done.4.refs_1_ = bf16[2,2,2,64,256]{4,3,2,1,0:T(8,128)(2,1)S(1)} collective-permute-done((bf16[2,2,2,64,256]{4,3,2,1,0:T(8,128)(2,1)S(1)}, bf16[2,2,2,64,256]{4,3,2,1,0:T(8,128)(2,1)S(1)}, u32[]{:S(2)}, u32[]{:S(2)}) %collective-permute-start.4) | collective-permute-done | bytes 262176 | tf_op jit(solution)/shard_map/ppermute | solution.py:461
  23.8 4.7 %collective-permute-done.3.refs_0_ = bf16[2,2,2,64,256]{4,3,2,1,0:T(8,128)(2,1)S(1)} collective-permute-done((bf16[2,2,2,64,256]{4,3,2,1,0:T(8,128)(2,1)S(1)}, bf16[2,2,2,64,256]{4,3,2,1,0:T(8,128)(2,1)S(1)}, u32[]{:S(2)}, u32[]{:S(2)}) %collective-permute-start.3) | collective-permute-done | bytes 262176 | tf_op jit(solution)/shard_map/ppermute | solution.py:461
  28.5 0.1 groups.1.mine
  28.6 0.1 collective-permute-start.7
  28.8 1.4 %rolled.1 = (bf16[2,512,512]{2,1,0:T(8,128)(2,1)S(1)}, bf16[2,512,256]{2,1,0:T(8,128)(2,1)S(1)}, bf16[2,256,512]{2,1,0:T(8,128)(2,1)S(1)}) custom-call(bf16[272,512]{1,0:T(8,128)(2,1)S(1)} %collective-permute-done.2.notes.refs_0_, bf16[2,512,512]{2,1,0:T(8,128)(2,1)S(1)} %copy-done.3, bf16[2,512,512]{2,1,0:T(8,128)(2,1)S(1)} %copy-done.5, ...), custom_call_target="tpu_custom_call" | custom-call | flops 8589934592 | bytes 6291456 | tf_op jit(solution)/shard_map/rolled/pallas_call | solution.py:133
  30.3 1.5 %collective-permute-done.7.theirs = bf16[5,2,2,2,64,256]{5,4,3,2,1,0:T(8,128)(2,1)S(1)} collective-permute-done((bf16[5,2,2,2,64,256]{5,4,3,2,1,0:T(8,128)(2,1)S(1)}, bf16[5,2,2,2,64,256]{5,4,3,2,1,0:T(8,128)(2,1)S(1)}, u32[]{:S(2)}, u32[]{:S(2)}) %collective-permute-start.7) | collective-permute-done | bytes 1310752 | tf_op jit(solution)/shard_map/ppermute | solution.py:461
  31.7 0.1 forth.1
  31.9 8.3 %collective-permute-done.8.refs_1_ = bf16[256,512]{1,0:T(8,128)(2,1)S(1)} collective-permute-done((bf16[256,512]{1,0:T(8,128)(2,1)S(1)}, bf16[256,512]{1,0:T(8,128)(2,1)S(1)}, u32[]{:S(2)}, u32[]{:S(2)}) %collective-permute-start.8) | collective-permute-done | bytes 262176 | tf_op jit(solution)/shard_map/ppermute | solution.py:479
  40.1 0.3 back.1
  40.5 3.0 %collective-permute-done.9.got = bf16[5,2,2,2,64,256]{5,4,3,2,1,0:T(8,128)(2,1)S(1)} collective-permute-done((bf16[5,2,2,2,64,256]{5,4,3,2,1,0:T(8,128)(2,1)S(1)}, bf16[5,2,2,2,64,256]{5,4,3,2,1,0:T(8,128)(2,1)S(1)}, u32[]{:S(2)}, u32[]{:S(2)}) %collective-permute-start.9) | collective-permute-done | bytes 1310752 | tf_op jit(solution)/shard_map/ppermute | solution.py:461
  43.5 0.3 merge.1
  43.9 4.7 %collective-permute-start.11 = (bf16[2,2,2,64,256]{4,3,2,1,0:T(8,128)(2,1)S(1)}, bf16[2,2,2,64,256]{4,3,2,1,0:T(8,128)(2,1)S(1)}, u32[]{:S(2)}, u32[]{:S(2)}) collective-permute-start(bf16[2,2,2,64,256]{4,3,2,1,0:T(8,128)(2,1)S(1)} %get-tuple-element.50), channel_id=1, source_target_pairs={{0,8},{2,10},{4,12},{6,14},{8,0},{10,2},{12,4},{14,6},{16,24},{18,... | collective-permute-start | bytes 786440 | tf_op jit(solution)/shard_map/ppermute | solution.py:461
  48.6 0.5 collective-permute-start.13
  49.1 5.4 %collective-permute-done.13.got = bf16[2,2,64,256]{3,2,1,0:T(8,128)(2,1)S(1)} collective-permute-done((bf16[2,2,64,256]{3,2,1,0:T(8,128)(2,1)S(1)}, bf16[2,2,64,256]{3,2,1,0:T(8,128)(2,1)S(1)}, u32[]{:S(2)}, u32[]{:S(2)}) %collective-permute-start.13) | collective-permute-done | bytes 131104 | tf_op jit(solution)/shard_map/ppermute | solution.py:520
  54.6 0.3 collective-permute-done.11.refs_1_
  54.9 0.1 sums.1
  55.1 0.6 collective-permute-start.14
  55.7 0.3 collective-permute-done.15
  56.0 4.8 %collective-permute-done.14 = bf16[2,2,64,256]{3,2,1,0:T(8,128)(2,1)S(1)} collective-permute-done((bf16[2,2,64,256]{3,2,1,0:T(8,128)(2,1)S(1)}, bf16[2,2,64,256]{3,2,1,0:T(8,128)(2,1)S(1)}, u32[]{:S(2)}, u32[]{:S(2)}) %collective-permute-start.14) | collective-permute-done | bytes 131104 | tf_op jit(solution)/shard_map/ppermute | solution.py:531
  60.8 0.7 %convert_add_fusion = f32[2,2,64,256]{3,2,1,0:T(8,128)} fusion(bf16[2,2,64,256]{3,2,1,0:T(8,128)(2,1)S(1)} %collective-permute-done.15, f32[2,2,64,256]{3,2,1,0:T(8,128)S(1)} %get-tuple-element.56, bf16[2,2,64,256]{3,2,1,0:T(8,128)(2,1)S(1)} %collective-permute-done.14), kind=kLoop, calls=%fused_computation | loop fusion | flops 262144 | bytes 786432 | tf_op jit(solution)/shard_map/add | solution.py:532
  (23 shorter events, 0.3 us)
Async XLA Ops:
  1.0 7.8 %collective-permute-start = (bf16[2,2,64,256]{3,2,1,0:T(8,128)(2,1)S(1)}, bf16[2,2,64,256]{3,2,1,0:T(8,128)(2,1)S(1)}, u32[]{:S(2)}, u32[]{:S(2)}) collective-permute-start(bf16[2,2,64,256]{3,2,1,0:T(8,128)(2,1)S(1)} %convert_element_type.9.refs_0_), channel_id=1, source_target_pairs={{0,1},{1,0},{2,3},{3,2},{4,5},{5,4},{6,7},{7,6},{8,9},{9,8},{10,11... | collective-permute-start | bytes 393224 | tf_op jit(solution)/shard_map/ppermute | solution.py:473
  4.6 1.2 %copy-start = (f32[2,256,512]{2,1,0:T(8,128)S(1)}, f32[2,256,512]{2,1,0:T(8,128)}, u32[]{:S(2)}) copy-start(f32[2,256,512]{2,1,0:T(8,128)} %amps.1) | copy-start | bytes 3145732
  5.9 0.7 %copy-start.1 = (s32[2]{0:T(128)S(1)}, s32[2]{0:T(128)}, u32[]{:S(2)}) copy-start(s32[2]{0:T(128)} %offsets.1) | copy-start | bytes 28
  7.1 11.5 %collective-permute-start.2 = (bf16[272,512]{1,0:T(8,128)(2,1)S(1)}, bf16[272,512]{1,0:T(8,128)(2,1)S(1)}, u32[]{:S(2)}, u32[]{:S(2)}) collective-permute-start(bf16[272,512]{1,0:T(8,128)(2,1)S(1)} %get-tuple-element.34), channel_id=1, source_target_pairs={{0,8},{2,10},{4,12},{6,14},{8,16},{10,18},{12,20},{14,22},{16,24},... | collective-permute-start | bytes 835592 | tf_op jit(solution)/shard_map/ppermute | solution.py:458
  8.7 13.3 %collective-permute-start.1 = (bf16[2,512,256]{2,1,0:T(8,128)(2,1)}, bf16[2,512,256]{2,1,0:T(8,128)(2,1)S(1)}, u32[]{:S(2)}, u32[]{:S(2)}) collective-permute-start(bf16[2,512,256]{2,1,0:T(8,128)(2,1)} %refs_0_), channel_id=1, source_target_pairs={{0,1},{1,0},{2,3},{3,2},{4,5},{5,4},{6,7},{7,6},{8,9},{9,8},{10,11... | collective-permute-start | bytes 1572872 | tf_op jit(solution)/shard_map/ppermute | solution.py:476
  9.3 19.5 %copy-start.2 = (bf16[2,512,256]{2,1,0:T(8,128)(2,1)S(1)}, bf16[2,512,256]{2,1,0:T(8,128)(2,1)}, u32[]{:S(2)}) copy-start(bf16[2,512,256]{2,1,0:T(8,128)(2,1)} %refs_0_) | copy-start | bytes 1572868
  9.3 19.5 %copy-start.3 = (bf16[2,512,512]{2,1,0:T(8,128)(2,1)S(1)}, bf16[2,512,512]{2,1,0:T(8,128)(2,1)}, u32[]{:S(2)}) copy-start(bf16[2,512,512]{2,1,0:T(8,128)(2,1)} %constant.6.clone.far_rows) | copy-start | bytes 3145732
  9.3 19.5 %copy-start.5 = (bf16[2,512,512]{2,1,0:T(8,128)(2,1)S(1)}, bf16[2,512,512]{2,1,0:T(8,128)(2,1)}, u32[]{:S(2)}) copy-start(bf16[2,512,512]{2,1,0:T(8,128)(2,1)} %constant.7.clone.far_cols) | copy-start | bytes 3145732
  9.3 12.7 %collective-permute-start.6 = (bf16[2,2,2,64,256]{4,3,2,1,0:T(8,128)(2,1)S(1)}, bf16[2,2,2,64,256]{4,3,2,1,0:T(8,128)(2,1)S(1)}, u32[]{:S(2)}, u32[]{:S(2)}) collective-permute-start(bf16[2,2,2,64,256]{4,3,2,1,0:T(8,128)(2,1)S(1)} %halves.1.refs_2_), channel_id=1, source_target_pairs={{0,2},{2,0},{4,6},{6,4},{8,16},{10,18},{12,20},{14,22},{16,8},{18,... | collective-permute-start | bytes 786440 | tf_op jit(solution)/shard_map/ppermute | solution.py:468
  9.4 12.6 %collective-permute-start.5 = (bf16[2,2,2,64,256]{4,3,2,1,0:T(8,128)(2,1)S(1)}, bf16[2,2,2,64,256]{4,3,2,1,0:T(8,128)(2,1)S(1)}, u32[]{:S(2)}, u32[]{:S(2)}) collective-permute-start(bf16[2,2,2,64,256]{4,3,2,1,0:T(8,128)(2,1)S(1)} %halves.1.refs_2_), channel_id=1, source_target_pairs={{0,2},{2,0},{4,8},{6,10},{8,4},{10,6},{12,16},{14,18},{16,12},{18,... | collective-permute-start | bytes 786440 | tf_op jit(solution)/shard_map/ppermute | solution.py:468
  9.9 13.9 %collective-permute-start.4 = (bf16[2,2,2,64,256]{4,3,2,1,0:T(8,128)(2,1)S(1)}, bf16[2,2,2,64,256]{4,3,2,1,0:T(8,128)(2,1)S(1)}, u32[]{:S(2)}, u32[]{:S(2)}) collective-permute-start(bf16[2,2,2,64,256]{4,3,2,1,0:T(8,128)(2,1)S(1)} %halves.1.refs_2_), channel_id=1, source_target_pairs={{0,4},{2,6},{4,0},{6,2},{8,12},{10,14},{12,8},{14,10},{16,20},{18,... | collective-permute-start | bytes 786440 | tf_op jit(solution)/shard_map/ppermute | solution.py:461
  18.6 9.9 %collective-permute-start.3 = (bf16[2,2,2,64,256]{4,3,2,1,0:T(8,128)(2,1)S(1)}, bf16[2,2,2,64,256]{4,3,2,1,0:T(8,128)(2,1)S(1)}, u32[]{:S(2)}, u32[]{:S(2)}) collective-permute-start(bf16[2,2,2,64,256]{4,3,2,1,0:T(8,128)(2,1)S(1)} %halves.1.refs_2_), channel_id=1, source_target_pairs={{0,8},{2,10},{4,12},{6,14},{8,0},{10,2},{12,4},{14,6},{16,24},{18,... | collective-permute-start | bytes 786440 | tf_op jit(solution)/shard_map/ppermute | solution.py:461
  28.6 3.1 %collective-permute-start.7 = (bf16[5,2,2,2,64,256]{5,4,3,2,1,0:T(8,128)(2,1)S(1)}, bf16[5,2,2,2,64,256]{5,4,3,2,1,0:T(8,128)(2,1)S(1)}, u32[]{:S(2)}, u32[]{:S(2)}) collective-permute-start(bf16[5,2,2,2,64,256]{5,4,3,2,1,0:T(8,128)(2,1)S(1)} %groups.1.mine), channel_id=1, source_target_pairs={{0,2},{2,0},{4,6},{6,4},{8,10},{10,8},{12,14},{14,12},{16,18},{18,... | collective-permute-start | bytes 3932168 | tf_op jit(solution)/shard_map/ppermute | solution.py:461
  28.8 3.0 %copy-start.4 = (bf16[2,512,512]{2,1,0:T(8,128)(2,1)S(1)}, bf16[2,512,512]{2,1,0:T(8,128)(2,1)}, u32[]{:S(2)}) copy-start(bf16[2,512,512]{2,1,0:T(8,128)(2,1)} %constant.8.clone.near) | copy-start | bytes 3145732
  28.8 11.4 %collective-permute-start.8 = (bf16[256,512]{1,0:T(8,128)(2,1)S(1)}, bf16[256,512]{1,0:T(8,128)(2,1)S(1)}, u32[]{:S(2)}, u32[]{:S(2)}) collective-permute-start(bf16[256,512]{1,0:T(8,128)(2,1)S(1)} %get-tuple-element.43), channel_id=1, source_target_pairs={{0,9},{1,8},{2,11},{3,10},{4,13},{5,12},{6,15},{7,14},{8,17},{9,16... | collective-permute-start | bytes 786440 | tf_op jit(solution)/shard_map/ppermute | solution.py:479
  40.4 3.1 %collective-permute-start.9 = (bf16[5,2,2,2,64,256]{5,4,3,2,1,0:T(8,128)(2,1)S(1)}, bf16[5,2,2,2,64,256]{5,4,3,2,1,0:T(8,128)(2,1)S(1)}, u32[]{:S(2)}, u32[]{:S(2)}) collective-permute-start(bf16[5,2,2,2,64,256]{5,4,3,2,1,0:T(8,128)(2,1)S(1)} %get-tuple-element.48), channel_id=1, source_target_pairs={{0,2},{2,0},{4,6},{6,4},{8,10},{10,8},{12,14},{14,12},{16,18},{18,... | collective-permute-start | bytes 3932168 | tf_op jit(solution)/shard_map/ppermute | solution.py:461
  43.8 10.8 %collective-permute-start.10 = (bf16[2,2,2,64,256]{4,3,2,1,0:T(8,128)(2,1)S(1)}, bf16[2,2,2,64,256]{4,3,2,1,0:T(8,128)(2,1)S(1)}, u32[]{:S(2)}, u32[]{:S(2)}) collective-permute-start(bf16[2,2,2,64,256]{4,3,2,1,0:T(8,128)(2,1)S(1)} %get-tuple-element.49), channel_id=1, source_target_pairs={{0,4},{2,6},{4,0},{6,2},{8,12},{10,14},{12,8},{14,10},{16,20},{18,... | collective-permute-start | bytes 786440 | tf_op jit(solution)/shard_map/ppermute | solution.py:461
  43.9 11.0 %collective-permute-start.11 = (bf16[2,2,2,64,256]{4,3,2,1,0:T(8,128)(2,1)S(1)}, bf16[2,2,2,64,256]{4,3,2,1,0:T(8,128)(2,1)S(1)}, u32[]{:S(2)}, u32[]{:S(2)}) collective-permute-start(bf16[2,2,2,64,256]{4,3,2,1,0:T(8,128)(2,1)S(1)} %get-tuple-element.50), channel_id=1, source_target_pairs={{0,8},{2,10},{4,12},{6,14},{8,0},{10,2},{12,4},{14,6},{16,24},{18,... | collective-permute-start | bytes 786440 | tf_op jit(solution)/shard_map/ppermute | solution.py:461
  48.6 6.3 %collective-permute-start.12 = (bf16[2,2,2,64,256]{4,3,2,1,0:T(8,128)(2,1)S(1)}, bf16[2,2,2,64,256]{4,3,2,1,0:T(8,128)(2,1)S(1)}, u32[]{:S(2)}, u32[]{:S(2)}) collective-permute-start(bf16[2,2,2,64,256]{4,3,2,1,0:T(8,128)(2,1)S(1)} %get-tuple-element.51), channel_id=1, source_target_pairs={{0,2},{2,0},{4,6},{6,4},{8,16},{10,18},{12,20},{14,22},{16,8},{18,... | collective-permute-start | bytes 786440 | tf_op jit(solution)/shard_map/ppermute | solution.py:468
  48.6 5.9 %collective-permute-start.13 = (bf16[2,2,64,256]{3,2,1,0:T(8,128)(2,1)S(1)}, bf16[2,2,64,256]{3,2,1,0:T(8,128)(2,1)S(1)}, u32[]{:S(2)}, u32[]{:S(2)}) collective-permute-start(bf16[2,2,64,256]{3,2,1,0:T(8,128)(2,1)S(1)} %get-tuple-element.54), channel_id=1, source_target_pairs={{0,1},{1,0},{2,3},{3,2},{4,5},{5,4},{6,7},{7,6},{8,9},{9,8},{10,11... | collective-permute-start | bytes 393224 | tf_op jit(solution)/shard_map/ppermute | solution.py:520
  54.6 1.4 %collective-permute-start.15 = (bf16[2,2,64,256]{3,2,1,0:T(8,128)(2,1)S(1)}, bf16[2,2,64,256]{3,2,1,0:T(8,128)(2,1)S(1)}, u32[]{:S(2)}, u32[]{:S(2)}) collective-permute-start(bf16[2,2,64,256]{3,2,1,0:T(8,128)(2,1)S(1)} %near.3), channel_id=1, source_target_pairs={{0,2},{2,0},{4,8},{6,10},{8,4},{10,6},{12,16},{14,18},{16,12},{18,... | collective-permute-start | bytes 393224 | tf_op jit(solution)/shard_map/ppermute | solution.py:468
  55.1 5.7 %collective-permute-start.14 = (bf16[2,2,64,256]{3,2,1,0:T(8,128)(2,1)S(1)}, bf16[2,2,64,256]{3,2,1,0:T(8,128)(2,1)S(1)}, u32[]{:S(2)}, u32[]{:S(2)}) collective-permute-start(bf16[2,2,64,256]{3,2,1,0:T(8,128)(2,1)S(1)} %get-tuple-element.57), channel_id=1, source_target_pairs={{0,1},{1,0},{2,3},{3,2},{4,5},{5,4},{6,7},{7,6},{8,9},{9,8},{10,11... | collective-permute-start | bytes 393224 | tf_op jit(solution)/shard_map/ppermute | solution.py:531
